TPU v7x, 32 devices: a whole 2x2x4 slice. The times are simulated.
32 devices in a mesh: gx: 4 (over z), gy: 2 (over x), gz: 4 (over y, core).
Axes of the slice: x: 2, y: 2, z: 4, core: 2. Of those that a mesh axis runs over, the one named last changes fastest.
Arguments:
- start_block: bfloat16 [24, 12, 96, 128], P('gx', 'gy', 'gz'), may hold values from -60 to 60
- locked_orbitals: bfloat16 [24, 12, 96, 384], P('gx', 'gy', 'gz'), may hold values from -5 to 5
- cell_h: bfloat16 [4, 2, 16, 343, 343], P('gx', 'gy', 'gz'), may hold values from -1 to 4, as said below
Outputs:
- orbitals: float32 [24, 12, 96, 128], P('gx', 'gy', 'gz')
Inputs may be any that keep to these rules, and one draw needn't show every extreme that they name: `cell_h`: every cell matrix is symmetric.
All inputs are finite; a program needn't handle non-finite values.
Results may differ from a plain program's by a relative error of at most 0.0042.
Values may be sent and summed in bfloat16 or wider, within the bound.
A program may use at most 64 MiB of HBM per device.

v0:
```python
import jax
import jax.numpy as jnp
from jax import lax
from jax.sharding import PartitionSpec as P

ORDER = 6
NODE = 343
APPLY = 6
LOCKED = 384


filter_low = 3.0
filter_high = 40.0
filter_bottom = 0.5


def padded_2(cells, sides, width):
    for axis, dim in sides:
        count = lax.axis_size(axis)
        head = lax.slice_in_dim(cells, 0, width, axis=dim)
        tail = lax.slice_in_dim(cells, cells.shape[dim] - width, cells.shape[dim], axis=dim)
        cells = jnp.concatenate(
            [
                lax.ppermute(tail, axis, [(i, (i + 1) % count) for i in range(count)]),
                cells,
                lax.ppermute(head, axis, [((i + 1) % count, i) for i in range(count)]),
            ],
            axis=dim,
        )
    return cells


def passed_along(block, axis, distance):
    devices = range(lax.axis_size(axis))
    route = [((i - distance) % len(devices), i) for i in devices]
    return lax.ppermute(block, axis, route)


def split_cells(grown, axis_pos, cell_count):
    head_part = lax.slice_in_dim(grown, 0, ORDER * cell_count, axis=axis_pos)
    head_part = head_part.reshape(
        grown.shape[:axis_pos] + (cell_count, ORDER) + grown.shape[axis_pos + 1 :]
    )
    tail_part = lax.slice_in_dim(grown, ORDER, ORDER * cell_count + 1, stride=ORDER, axis=axis_pos)
    tail_part = jnp.expand_dims(tail_part, axis_pos + 1)
    return jnp.concatenate([head_part, tail_part], axis_pos + 1)


def merge_cells(cell_local, axis_pos, cell_count):
    new_shape = (
        cell_local.shape[:axis_pos] + (cell_count * ORDER,) + cell_local.shape[axis_pos + 2 :]
    )
    head_part = lax.slice_in_dim(cell_local, 0, ORDER, axis=axis_pos + 1).reshape(new_shape)
    tail_part = lax.slice_in_dim(cell_local, ORDER, ORDER + 1, axis=axis_pos + 1)
    zero_tail = jnp.zeros(
        cell_local.shape[: axis_pos + 1] + (ORDER - 1,) + cell_local.shape[axis_pos + 2 :],
        cell_local.dtype,
    )
    tail_part = jnp.concatenate([zero_tail, tail_part], axis_pos + 1).reshape(new_shape)
    zero_layer = jnp.zeros(
        cell_local.shape[:axis_pos] + (1,) + cell_local.shape[axis_pos + 2 :], cell_local.dtype
    )
    return jnp.concatenate([head_part, zero_layer], axis_pos) + jnp.concatenate(
        [zero_layer, tail_part], axis_pos
    )


def cell_terms(grown, cell_h):
    count_x, count_y, count_z = (cell_h.shape[0], cell_h.shape[1], cell_h.shape[2])
    block_width = grown.shape[3]
    cell_local = split_cells(grown, 0, count_x)
    cell_local = split_cells(cell_local, 2, count_y)
    cell_local = split_cells(cell_local, 4, count_z)
    cell_local = cell_local.transpose(0, 2, 4, 1, 3, 5, 6).reshape(
        count_x, count_y, count_z, NODE, block_width
    )
    products = jnp.einsum(
        "abcij,abcjv->abciv", cell_h, cell_local, preferred_element_type=jnp.float32
    )
    side = ORDER + 1
    products = products.reshape(count_x, count_y, count_z, side, side, side, block_width).transpose(
        0, 3, 1, 4, 2, 5, 6
    )
    products = merge_cells(products, 4, count_z)
    products = merge_cells(products, 2, count_y)
    return merge_cells(products, 0, count_x)


def fold_rims(padded, axis_pos):
    total = padded.shape[axis_pos]
    inner = lax.slice_in_dim(padded, 1, total - 1, axis=axis_pos)
    low_rim = lax.slice_in_dim(padded, 0, 1, axis=axis_pos)
    high_rim = lax.slice_in_dim(padded, total - 1, total, axis=axis_pos)
    first_row = lax.slice_in_dim(inner, 0, 1, axis=axis_pos) + low_rim
    last_row = lax.slice_in_dim(inner, total - 3, total - 2, axis=axis_pos) + high_rim
    middle = lax.slice_in_dim(inner, 1, total - 3, axis=axis_pos)
    return jnp.concatenate([first_row, middle, last_row], axis_pos)


def apply_operator(values, cell_h):
    terms = cell_terms(values.astype(jnp.bfloat16), cell_h)
    padded = padded_2(terms, (("gx", 0), ("gy", 1), ("gz", 2)), 1)
    terms = fold_rims(fold_rims(fold_rims(padded, 0), 1), 2)
    return terms


def normalize(gram_matrix, vectors):
    factor = jnp.linalg.cholesky(gram_matrix)
    inverse = jax.scipy.linalg.solve_triangular(
        factor, jnp.eye(gram_matrix.shape[0], dtype=jnp.float32), lower=True
    )
    return jnp.dot(
        vectors, inverse.T, precision=lax.Precision.HIGHEST, preferred_element_type=jnp.float32
    )


def per_device(start_block, locked_orbitals, cell_h):
    devices = lax.axis_size("gx") * lax.axis_size("gy") * lax.axis_size("gz")
    block_width = start_block.shape[3]
    nodes_total = float(
        start_block.shape[0] * start_block.shape[1] * start_block.shape[2] * devices
    )
    rim_first = passed_along(start_block[0:1], "gx", -1)
    grown = jnp.concatenate([start_block, rim_first], 0)
    rim_second = passed_along(grown[:, 0:1], "gy", -1)
    grown = jnp.concatenate([grown, rim_second], 1)
    rim_third = passed_along(grown[:, :, 0:1], "gz", -1)
    grown = jnp.concatenate([grown, rim_third], 2)
    half_span = (filter_high - filter_low) / 2.0
    center = (filter_high + filter_low) / 2.0
    sigma_first = half_span / (filter_bottom - center)
    previous = grown.astype(jnp.float32)
    current = sigma_first / half_span * (apply_operator(grown, cell_h) - center * previous)
    sigma_now = sigma_first
    for repeat in range(APPLY - 1):
        sigma_next = 1.0 / (2.0 / sigma_first - sigma_now)
        following = (
            2.0 * sigma_next / half_span * (apply_operator(current, cell_h) - center * current)
            - sigma_now * sigma_next * previous
        )
        previous = current
        current = following
        sigma_now = sigma_next
    filtered = current[:-1, :-1, :-1].astype(jnp.bfloat16).reshape(-1, block_width)
    locked_flat = locked_orbitals.reshape(-1, LOCKED)
    contract = (((0,), (0,)), ((), ()))
    cross_part = lax.dot_general(
        locked_flat, filtered, contract, preferred_element_type=jnp.float32
    )
    self_part = lax.dot_general(filtered, filtered, contract, preferred_element_type=jnp.float32)
    locked_part = lax.dot_general(
        locked_flat, locked_flat, contract, preferred_element_type=jnp.float32
    )
    cross, self_gram, locked_gram = lax.psum(
        (cross_part, self_part, locked_part), ("gx", "gy", "gz")
    )
    coefficient = (cross / nodes_total).astype(jnp.bfloat16)
    coef_wide = coefficient.astype(jnp.float32)
    projected = filtered.astype(jnp.float32) - jnp.dot(
        locked_flat, coefficient, preferred_element_type=jnp.float32
    )
    mixed = lax.dot_general(
        cross,
        coef_wide,
        contract,
        precision=lax.Precision.HIGHEST,
        preferred_element_type=jnp.float32,
    )
    weighted = jnp.dot(
        locked_gram, coef_wide, precision=lax.Precision.HIGHEST, preferred_element_type=jnp.float32
    )
    quadratic = lax.dot_general(
        coef_wide,
        weighted,
        contract,
        precision=lax.Precision.HIGHEST,
        preferred_element_type=jnp.float32,
    )
    gram_matrix = (self_gram - mixed - mixed.T + quadratic) / nodes_total
    result = normalize(gram_matrix, projected)
    return result.reshape(start_block.shape)


def solution(mesh):
    placed = (P("gx", "gy", "gz", None), P("gx", "gy", "gz", None), P("gx", "gy", "gz", None, None))
    return jax.shard_map(
        per_device, mesh=mesh, in_specs=placed, out_specs=P("gx", "gy", "gz", None), check_vma=False
    )
```

profile of v0, /device:TPU:0, one launch (start us, length us, event | category | flops | bytes accessed | tf_op | source)
XLA Modules:
  0.0 360.3 jit_solution(1890642727778564677)
XLA Ops:
  7.4 5.0 %collective-permute-start = (bf16[1,6,24,128]{3,2,1,0:T(8,128)(2,1)S(1)}, bf16[1,6,24,128]{3,2,1,0:T(8,128)(2,1)S(1)}, u32[]{:S(2)}, u32[]{:S(2)}) collective-permute-start(bf16[1,6,24,128]{3,2,1,0:T(8,128)(2,1)S(1)} %slice.703), channel_id=1, source_target_pairs={{8,0},{16,8},{24,16},{0,24},{9,1},{17,9},{25,17},{1,25},{10,2},{18... | collective-permute-start | bytes 110600 | tf_op jit(solution)/shard_map/ppermute | solution.py:36
  14.1 1.6 collective-permute-start.1
  15.7 2.5 collective-permute-done.1
  18.3 1.5 collective-permute-done.2
  23.3 3.9 %collective-permute-start.4 = (f32[1,7,25,128]{3,2,1,0:T(8,128)S(1)}, f32[1,7,25,128]{3,2,1,0:T(8,128)S(1)}, u32[]{:S(2)}, u32[]{:S(2)}) collective-permute-start(f32[1,7,25,128]{3,2,1,0:T(8,128)S(1)} %get-tuple-element.25), channel_id=1, source_target_pairs={{8,0},{16,8},{24,16},{0,24},{9,1},{17,9},{25,17},{1,25},{10,2},{18... | collective-permute-start | bytes 268808 | tf_op jit(solution)/shard_map/ppermute | solution.py:26
  27.3 3.0 collective-permute-done.3
  31.3 1.6 collective-permute-start.5
  33.4 4.6 %collective-permute-done.5 = f32[9,1,25,128]{3,2,1,0:T(8,128)S(1)} collective-permute-done((f32[9,1,25,128]{3,2,1,0:T(8,128)S(1)}, f32[9,1,25,128]{3,2,1,0:T(8,128)S(1)}, u32[]{:S(2)}, u32[]{:S(2)}) %collective-permute-start.5) | collective-permute-done | bytes 115232 | tf_op jit(solution)/shard_map/ppermute | solution.py:24
  38.0 2.5 collective-permute-done.6
  40.7 1.7 collective-permute-start.8
  42.4 1.7 collective-permute-done.7
  48.2 2.6 collective-permute-start.9
  50.9 1.3 collective-permute-start.10
  52.3 3.4 collective-permute-done.9
  55.7 2.8 collective-permute-done.10
  58.5 1.6 collective-permute-start.11
  60.6 4.7 %collective-permute-done.11 = f32[9,1,25,128]{3,2,1,0:T(8,128)S(1)} collective-permute-done((f32[9,1,25,128]{3,2,1,0:T(8,128)S(1)}, f32[9,1,25,128]{3,2,1,0:T(8,128)S(1)}, u32[]{:S(2)}, u32[]{:S(2)}) %collective-permute-start.11) | collective-permute-done | bytes 115232 | tf_op jit(solution)/shard_map/ppermute | solution.py:24
  65.3 2.3 collective-permute-done.12
  67.7 1.9 collective-permute-start.14
  69.6 1.5 collective-permute-done.13
  73.5 3.4 slice.777
  80.1 3.2 collective-permute-start.16
  83.5 3.8 %collective-permute-done.15 = f32[1,7,25,128]{3,2,1,0:T(8,128)S(1)} collective-permute-done((f32[1,7,25,128]{3,2,1,0:T(8,128)S(1)}, f32[1,7,25,128]{3,2,1,0:T(8,128)S(1)}, u32[]{:S(2)}, u32[]{:S(2)}) %collective-permute-start.15) | collective-permute-done | bytes 89632 | tf_op jit(solution)/shard_map/ppermute | solution.py:24
  87.2 1.3 collective-permute-done.16
  88.6 1.6 collective-permute-start.17
  90.7 4.7 %collective-permute-done.17 = f32[9,1,25,128]{3,2,1,0:T(8,128)S(1)} collective-permute-done((f32[9,1,25,128]{3,2,1,0:T(8,128)S(1)}, f32[9,1,25,128]{3,2,1,0:T(8,128)S(1)}, u32[]{:S(2)}, u32[]{:S(2)}) %collective-permute-start.17) | collective-permute-done | bytes 115232 | tf_op jit(solution)/shard_map/ppermute | solution.py:24
  95.3 2.3 collective-permute-done.18
  97.8 1.7 collective-permute-start.20
  99.5 1.7 collective-permute-done.19
  104.4 4.3 %slice.810 = bf16[1,7,1,7,4,128]{5,4,3,1,2,0:T(4,128)(2,1)} slice(bf16[1,7,1,7,25,128]{5,4,3,1,2,0:T(8,128)(2,1)} %pad_maximum_fusion.21), slice={[0:1:1], [0:7:1], [0:1:1], [0:7:1], [6:25:6], [0:128:1]} | slice | bytes 100352 | tf_op jit(solution)/shard_map/slice | solution.py:44
  109.5 1.0 copy.78
  113.7 3.2 collective-permute-start.22
  117.0 3.9 %collective-permute-done.21 = f32[1,7,25,128]{3,2,1,0:T(8,128)S(1)} collective-permute-done((f32[1,7,25,128]{3,2,1,0:T(8,128)S(1)}, f32[1,7,25,128]{3,2,1,0:T(8,128)S(1)}, u32[]{:S(2)}, u32[]{:S(2)}) %collective-permute-start.21) | collective-permute-done | bytes 89632 | tf_op jit(solution)/shard_map/ppermute | solution.py:24
  121.9 1.6 collective-permute-start.23
  124.0 4.7 %collective-permute-done.23 = f32[9,1,25,128]{3,2,1,0:T(8,128)S(1)} collective-permute-done((f32[9,1,25,128]{3,2,1,0:T(8,128)S(1)}, f32[9,1,25,128]{3,2,1,0:T(8,128)S(1)}, u32[]{:S(2)}, u32[]{:S(2)}) %collective-permute-start.23) | collective-permute-done | bytes 115232 | tf_op jit(solution)/shard_map/ppermute | solution.py:24
  128.6 2.3 collective-permute-done.24
  131.1 1.9 collective-permute-start.26
  133.0 1.5 collective-permute-done.25
  135.5 1.7 fusion.100
  140.2 1.8 collective-permute-start.27
  142.1 2.0 collective-permute-start.28
  144.2 3.9 %collective-permute-done.27 = f32[1,7,25,128]{3,2,1,0:T(8,128)S(1)} collective-permute-done((f32[1,7,25,128]{3,2,1,0:T(8,128)S(1)}, f32[1,7,25,128]{3,2,1,0:T(8,128)S(1)}, u32[]{:S(2)}, u32[]{:S(2)}) %collective-permute-start.27) | collective-permute-done | bytes 89632 | tf_op jit(solution)/shard_map/ppermute | solution.py:24
  148.1 2.1 collective-permute-done.28
  150.3 1.6 collective-permute-start.29
  152.4 4.7 %collective-permute-done.29 = f32[9,1,25,128]{3,2,1,0:T(8,128)S(1)} collective-permute-done((f32[9,1,25,128]{3,2,1,0:T(8,128)S(1)}, f32[9,1,25,128]{3,2,1,0:T(8,128)S(1)}, u32[]{:S(2)}, u32[]{:S(2)}) %collective-permute-start.29) | collective-permute-done | bytes 115232 | tf_op jit(solution)/shard_map/ppermute | solution.py:24
  157.1 2.0 collective-permute-done.30
  159.2 1.7 collective-permute-start.32
  160.9 1.7 collective-permute-done.31
  164.4 1.2 fusion.98
  169.1 3.4 collective-permute-start.34
  172.7 3.6 collective-permute-done.33
  176.3 1.1 collective-permute-done.34
  177.4 1.6 collective-permute-start.35
  179.5 4.7 %collective-permute-done.35 = f32[9,1,25,128]{3,2,1,0:T(8,128)S(1)} collective-permute-done((f32[9,1,25,128]{3,2,1,0:T(8,128)S(1)}, f32[9,1,25,128]{3,2,1,0:T(8,128)S(1)}, u32[]{:S(2)}, u32[]{:S(2)}) %collective-permute-start.35) | collective-permute-done | bytes 115232 | tf_op jit(solution)/shard_map/ppermute | solution.py:24
  184.2 2.3 collective-permute-done.36
  186.6 2.0 collective-permute-start.38
  188.6 1.4 convolution_bitcast_fusion.6
  193.1 1.0 convolution_bitcast_fusion.8
  194.2 130.6 %all-reduce.57.cloned.1.call-done = (f32[384,128]{0,1:T(8,128)}, f32[384,384]{1,0:T(8,128)}, f32[128,128]{0,1:T(8,128)}) async-done(((f32[384,128]{0,1:T(8,128)}, f32[384,384]{1,0:T(8,128)}, f32[128,128]{0,1:T(8,128)}), (f32[384,128]{0,1:T(8,128)}, f32[384,384]{1,0:T(8,128)}, f32[128,128]{0,1:T(8,128)})) %all-reduce.57.cloned.1.call-update) | async-done | bytes 851984 | tf_op jit(solution)/shard_map/psum | solution.py:154
  324.8 1.3 fusion.92
  326.1 1.5 fusion.91
  328.2 11.7 %cholesky.17 = f32[128,128]{1,0:T(8,128)S(1)} custom-call(f32[128,128]{1,0:T(8,128)S(1)} %fusion.84), custom_call_target="Cholesky" | custom-call | tf_op jit(solution)/shard_map/jit(cholesky)/cholesky | solution.py:108
  341.3 9.8 %custom-call.7 = f32[1,128,128]{1,2,0:T(8,128)S(1)} custom-call(f32[1,128,128]{2,1,0:T(8,128)S(1)} %fusion.81), custom_call_target="InvertDiagBlocksLowerTriangular" | custom-call | tf_op jit(solution)/shard_map/jit(_solve_triangular)/triangular_solve | solution.py:109
  351.7 1.3 fusion.104
  (279 shorter events, 42.8 us)
Async XLA Ops:
  6.5 14.2 %copy-start = (bf16[1,1,4,343,343]{4,2,3,1,0:T(4,128)(2,1)S(1)}, bf16[1,1,4,343,343]{4,2,3,1,0:T(4,128)(2,1)}, u32[]{:S(2)}) copy-start(bf16[1,1,4,343,343]{4,2,3,1,0:T(4,128)(2,1)} %param.5) | copy-start | bytes 2823580
  6.5 318.2 %all-reduce.57.cloned.1.call-start = ((), (), s32[]{:S(2)}) async-start(), calls=%async_computation | async-start | bytes 1703936 | tf_op jit(solution)/shard_map/psum | solution.py:154
  7.4 6.7 %collective-permute-start = (bf16[1,6,24,128]{3,2,1,0:T(8,128)(2,1)S(1)}, bf16[1,6,24,128]{3,2,1,0:T(8,128)(2,1)S(1)}, u32[]{:S(2)}, u32[]{:S(2)}) collective-permute-start(bf16[1,6,24,128]{3,2,1,0:T(8,128)(2,1)S(1)} %slice.703), channel_id=1, source_target_pairs={{8,0},{16,8},{24,16},{0,24},{9,1},{17,9},{25,17},{1,25},{10,2},{18... | collective-permute-start | bytes 110600 | tf_op jit(solution)/shard_map/ppermute | solution.py:36
  14.1 4.1 %collective-permute-start.1 = (bf16[7,1,24,128]{3,2,1,0:T(8,128)(2,1)S(1)}, bf16[7,1,24,128]{3,2,1,0:T(8,128)(2,1)S(1)}, u32[]{:S(2)}, u32[]{:S(2)}) collective-permute-start(bf16[7,1,24,128]{3,2,1,0:T(8,128)(2,1)S(1)} %slice.905), channel_id=1, source_target_pairs={{4,0},{0,4},{5,1},{1,5},{6,2},{2,6},{7,3},{3,7},{12,8},{8,12},{13,... | collective-permute-start | bytes 129032 | tf_op jit(solution)/shard_map/ppermute | solution.py:36
  18.2 1.6 collective-permute-start.2
  22.9 7.4 %collective-permute-start.3 = (f32[1,7,25,128]{3,2,1,0:T(8,128)S(1)}, f32[1,7,25,128]{3,2,1,0:T(8,128)S(1)}, u32[]{:S(2)}, u32[]{:S(2)}) collective-permute-start(f32[1,7,25,128]{3,2,1,0:T(8,128)S(1)} %get-tuple-element.24), channel_id=1, source_target_pairs={{0,8},{8,16},{16,24},{24,0},{1,9},{9,17},{17,25},{25,1},{2,10},{10... | collective-permute-start | bytes 268808 | tf_op jit(solution)/shard_map/ppermute | solution.py:24
  23.3 8.0 %collective-permute-start.4 = (f32[1,7,25,128]{3,2,1,0:T(8,128)S(1)}, f32[1,7,25,128]{3,2,1,0:T(8,128)S(1)}, u32[]{:S(2)}, u32[]{:S(2)}) collective-permute-start(f32[1,7,25,128]{3,2,1,0:T(8,128)S(1)} %get-tuple-element.25), channel_id=1, source_target_pairs={{8,0},{16,8},{24,16},{0,24},{9,1},{17,9},{25,17},{1,25},{10,2},{18... | collective-permute-start | bytes 268808 | tf_op jit(solution)/shard_map/ppermute | solution.py:26
  31.3 6.7 %collective-permute-start.5 = (f32[9,1,25,128]{3,2,1,0:T(8,128)S(1)}, f32[9,1,25,128]{3,2,1,0:T(8,128)S(1)}, u32[]{:S(2)}, u32[]{:S(2)}) collective-permute-start(f32[9,1,25,128]{3,2,1,0:T(8,128)S(1)} %get-tuple-element.60), channel_id=1, source_target_pairs={{0,4},{4,0},{1,5},{5,1},{2,6},{6,2},{3,7},{7,3},{8,12},{12,8},{9,1... | collective-permute-start | bytes 345608 | tf_op jit(solution)/shard_map/ppermute | solution.py:24
  32.9 7.7 %collective-permute-start.6 = (f32[9,1,25,128]{3,2,1,0:T(8,128)S(1)}, f32[9,1,25,128]{3,2,1,0:T(8,128)S(1)}, u32[]{:S(2)}, u32[]{:S(2)}) collective-permute-start(f32[9,1,25,128]{3,2,1,0:T(8,128)S(1)} %get-tuple-element.61), channel_id=1, source_target_pairs={{4,0},{0,4},{5,1},{1,5},{6,2},{2,6},{7,3},{3,7},{12,8},{8,12},{13,... | collective-permute-start | bytes 345608 | tf_op jit(solution)/shard_map/ppermute | solution.py:26
  40.6 3.5 collective-permute-start.7
  40.7 3.4 collective-permute-start.8
  48.2 7.5 %collective-permute-start.9 = (f32[1,7,25,128]{3,2,1,0:T(8,128)S(1)}, f32[1,7,25,128]{3,2,1,0:T(8,128)S(1)}, u32[]{:S(2)}, u32[]{:S(2)}) collective-permute-start(f32[1,7,25,128]{3,2,1,0:T(8,128)S(1)} %get-tuple-element.22), channel_id=1, source_target_pairs={{0,8},{8,16},{16,24},{24,0},{1,9},{9,17},{17,25},{25,1},{2,10},{10... | collective-permute-start | bytes 268808 | tf_op jit(solution)/shard_map/ppermute | solution.py:24
  50.9 7.6 %collective-permute-start.10 = (f32[1,7,25,128]{3,2,1,0:T(8,128)S(1)}, f32[1,7,25,128]{3,2,1,0:T(8,128)S(1)}, u32[]{:S(2)}, u32[]{:S(2)}) collective-permute-start(f32[1,7,25,128]{3,2,1,0:T(8,128)S(1)} %get-tuple-element.23), channel_id=1, source_target_pairs={{8,0},{16,8},{24,16},{0,24},{9,1},{17,9},{25,17},{1,25},{10,2},{18... | collective-permute-start | bytes 268808 | tf_op jit(solution)/shard_map/ppermute | solution.py:26
  58.5 6.8 %collective-permute-start.11 = (f32[9,1,25,128]{3,2,1,0:T(8,128)S(1)}, f32[9,1,25,128]{3,2,1,0:T(8,128)S(1)}, u32[]{:S(2)}, u32[]{:S(2)}) collective-permute-start(f32[9,1,25,128]{3,2,1,0:T(8,128)S(1)} %get-tuple-element.56), channel_id=1, source_target_pairs={{0,4},{4,0},{1,5},{5,1},{2,6},{6,2},{3,7},{7,3},{8,12},{12,8},{9,1... | collective-permute-start | bytes 345608 | tf_op jit(solution)/shard_map/ppermute | solution.py:24
  60.1 7.5 %collective-permute-start.12 = (f32[9,1,25,128]{3,2,1,0:T(8,128)S(1)}, f32[9,1,25,128]{3,2,1,0:T(8,128)S(1)}, u32[]{:S(2)}, u32[]{:S(2)}) collective-permute-start(f32[9,1,25,128]{3,2,1,0:T(8,128)S(1)} %get-tuple-element.57), channel_id=1, source_target_pairs={{4,0},{0,4},{5,1},{1,5},{6,2},{2,6},{7,3},{3,7},{12,8},{8,12},{13,... | collective-permute-start | bytes 345608 | tf_op jit(solution)/shard_map/ppermute | solution.py:26
  67.7 3.5 collective-permute-start.13
  67.7 3.6 collective-permute-start.14
  79.5 7.8 %collective-permute-start.15 = (f32[1,7,25,128]{3,2,1,0:T(8,128)S(1)}, f32[1,7,25,128]{3,2,1,0:T(8,128)S(1)}, u32[]{:S(2)}, u32[]{:S(2)}) collective-permute-start(f32[1,7,25,128]{3,2,1,0:T(8,128)S(1)} %get-tuple-element.20), channel_id=1, source_target_pairs={{0,8},{8,16},{16,24},{24,0},{1,9},{9,17},{17,25},{25,1},{2,10},{10... | collective-permute-start | bytes 268808 | tf_op jit(solution)/shard_map/ppermute | solution.py:24
  80.1 8.4 %collective-permute-start.16 = (f32[1,7,25,128]{3,2,1,0:T(8,128)S(1)}, f32[1,7,25,128]{3,2,1,0:T(8,128)S(1)}, u32[]{:S(2)}, u32[]{:S(2)}) collective-permute-start(f32[1,7,25,128]{3,2,1,0:T(8,128)S(1)} %get-tuple-element.21), channel_id=1, source_target_pairs={{8,0},{16,8},{24,16},{0,24},{9,1},{17,9},{25,17},{1,25},{10,2},{18... | collective-permute-start | bytes 268808 | tf_op jit(solution)/shard_map/ppermute | solution.py:26
  88.6 6.8 %collective-permute-start.17 = (f32[9,1,25,128]{3,2,1,0:T(8,128)S(1)}, f32[9,1,25,128]{3,2,1,0:T(8,128)S(1)}, u32[]{:S(2)}, u32[]{:S(2)}) collective-permute-start(f32[9,1,25,128]{3,2,1,0:T(8,128)S(1)} %get-tuple-element.52), channel_id=1, source_target_pairs={{0,4},{4,0},{1,5},{5,1},{2,6},{6,2},{3,7},{7,3},{8,12},{12,8},{9,1... | collective-permute-start | bytes 345608 | tf_op jit(solution)/shard_map/ppermute | solution.py:24
  90.1 7.5 %collective-permute-start.18 = (f32[9,1,25,128]{3,2,1,0:T(8,128)S(1)}, f32[9,1,25,128]{3,2,1,0:T(8,128)S(1)}, u32[]{:S(2)}, u32[]{:S(2)}) collective-permute-start(f32[9,1,25,128]{3,2,1,0:T(8,128)S(1)} %get-tuple-element.53), channel_id=1, source_target_pairs={{4,0},{0,4},{5,1},{1,5},{6,2},{2,6},{7,3},{3,7},{12,8},{8,12},{13,... | collective-permute-start | bytes 345608 | tf_op jit(solution)/shard_map/ppermute | solution.py:26
  97.7 3.5 collective-permute-start.19
  97.8 3.4 collective-permute-start.20
  113.0 7.9 %collective-permute-start.21 = (f32[1,7,25,128]{3,2,1,0:T(8,128)S(1)}, f32[1,7,25,128]{3,2,1,0:T(8,128)S(1)}, u32[]{:S(2)}, u32[]{:S(2)}) collective-permute-start(f32[1,7,25,128]{3,2,1,0:T(8,128)S(1)} %get-tuple-element.18), channel_id=1, source_target_pairs={{0,8},{8,16},{16,24},{24,0},{1,9},{9,17},{17,25},{25,1},{2,10},{10... | collective-permute-start | bytes 268808 | tf_op jit(solution)/shard_map/ppermute | solution.py:24
  113.7 8.2 %collective-permute-start.22 = (f32[1,7,25,128]{3,2,1,0:T(8,128)S(1)}, f32[1,7,25,128]{3,2,1,0:T(8,128)S(1)}, u32[]{:S(2)}, u32[]{:S(2)}) collective-permute-start(f32[1,7,25,128]{3,2,1,0:T(8,128)S(1)} %get-tuple-element.19), channel_id=1, source_target_pairs={{8,0},{16,8},{24,16},{0,24},{9,1},{17,9},{25,17},{1,25},{10,2},{18... | collective-permute-start | bytes 268808 | tf_op jit(solution)/shard_map/ppermute | solution.py:26
  121.9 6.8 %collective-permute-start.23 = (f32[9,1,25,128]{3,2,1,0:T(8,128)S(1)}, f32[9,1,25,128]{3,2,1,0:T(8,128)S(1)}, u32[]{:S(2)}, u32[]{:S(2)}) collective-permute-start(f32[9,1,25,128]{3,2,1,0:T(8,128)S(1)} %get-tuple-element.48), channel_id=1, source_target_pairs={{0,4},{4,0},{1,5},{5,1},{2,6},{6,2},{3,7},{7,3},{8,12},{12,8},{9,1... | collective-permute-start | bytes 345608 | tf_op jit(solution)/shard_map/ppermute | solution.py:24
  123.5 7.5 %collective-permute-start.24 = (f32[9,1,25,128]{3,2,1,0:T(8,128)S(1)}, f32[9,1,25,128]{3,2,1,0:T(8,128)S(1)}, u32[]{:S(2)}, u32[]{:S(2)}) collective-permute-start(f32[9,1,25,128]{3,2,1,0:T(8,128)S(1)} %get-tuple-element.49), channel_id=1, source_target_pairs={{4,0},{0,4},{5,1},{1,5},{6,2},{2,6},{7,3},{3,7},{12,8},{8,12},{13,... | collective-permute-start | bytes 345608 | tf_op jit(solution)/shard_map/ppermute | solution.py:26
  131.0 3.5 collective-permute-start.25
  131.1 3.6 collective-permute-start.26
  140.2 7.9 %collective-permute-start.27 = (f32[1,7,25,128]{3,2,1,0:T(8,128)S(1)}, f32[1,7,25,128]{3,2,1,0:T(8,128)S(1)}, u32[]{:S(2)}, u32[]{:S(2)}) collective-permute-start(f32[1,7,25,128]{3,2,1,0:T(8,128)S(1)} %get-tuple-element.16), channel_id=1, source_target_pairs={{0,8},{8,16},{16,24},{24,0},{1,9},{9,17},{17,25},{25,1},{2,10},{10... | collective-permute-start | bytes 268808 | tf_op jit(solution)/shard_map/ppermute | solution.py:24
  142.1 8.2 %collective-permute-start.28 = (f32[1,7,25,128]{3,2,1,0:T(8,128)S(1)}, f32[1,7,25,128]{3,2,1,0:T(8,128)S(1)}, u32[]{:S(2)}, u32[]{:S(2)}) collective-permute-start(f32[1,7,25,128]{3,2,1,0:T(8,128)S(1)} %get-tuple-element.17), channel_id=1, source_target_pairs={{8,0},{16,8},{24,16},{0,24},{9,1},{17,9},{25,17},{1,25},{10,2},{18... | collective-permute-start | bytes 268808 | tf_op jit(solution)/shard_map/ppermute | solution.py:26
  150.3 6.8 %collective-permute-start.29 = (f32[9,1,25,128]{3,2,1,0:T(8,128)S(1)}, f32[9,1,25,128]{3,2,1,0:T(8,128)S(1)}, u32[]{:S(2)}, u32[]{:S(2)}) collective-permute-start(f32[9,1,25,128]{3,2,1,0:T(8,128)S(1)} %get-tuple-element.44), channel_id=1, source_target_pairs={{0,4},{4,0},{1,5},{5,1},{2,6},{6,2},{3,7},{7,3},{8,12},{12,8},{9,1... | collective-permute-start | bytes 345608 | tf_op jit(solution)/shard_map/ppermute | solution.py:24
  151.8 7.2 %collective-permute-start.30 = (f32[9,1,25,128]{3,2,1,0:T(8,128)S(1)}, f32[9,1,25,128]{3,2,1,0:T(8,128)S(1)}, u32[]{:S(2)}, u32[]{:S(2)}) collective-permute-start(f32[9,1,25,128]{3,2,1,0:T(8,128)S(1)} %get-tuple-element.45), channel_id=1, source_target_pairs={{4,0},{0,4},{5,1},{1,5},{6,2},{2,6},{7,3},{3,7},{12,8},{8,12},{13,... | collective-permute-start | bytes 345608 | tf_op jit(solution)/shard_map/ppermute | solution.py:26
  159.1 3.5 collective-permute-start.31
  159.2 3.4 collective-permute-start.32
  163.3 1.1 copy-start.1
  168.6 7.6 %collective-permute-start.33 = (f32[1,7,25,128]{3,2,1,0:T(8,128)S(1)}, f32[1,7,25,128]{3,2,1,0:T(8,128)S(1)}, u32[]{:S(2)}, u32[]{:S(2)}) collective-permute-start(f32[1,7,25,128]{3,2,1,0:T(8,128)S(1)} %get-tuple-element.14), channel_id=1, source_target_pairs={{0,8},{8,16},{16,24},{24,0},{1,9},{9,17},{17,25},{25,1},{2,10},{10... | collective-permute-start | bytes 268808 | tf_op jit(solution)/shard_map/ppermute | solution.py:24
  169.1 8.3 %collective-permute-start.34 = (f32[1,7,25,128]{3,2,1,0:T(8,128)S(1)}, f32[1,7,25,128]{3,2,1,0:T(8,128)S(1)}, u32[]{:S(2)}, u32[]{:S(2)}) collective-permute-start(f32[1,7,25,128]{3,2,1,0:T(8,128)S(1)} %get-tuple-element.15), channel_id=1, source_target_pairs={{8,0},{16,8},{24,16},{0,24},{9,1},{17,9},{25,17},{1,25},{10,2},{18... | collective-permute-start | bytes 268808 | tf_op jit(solution)/shard_map/ppermute | solution.py:26
  172.7 15.9 %copy-start.3 = (bf16[6,6,24,384]{3,2,1,0:T(8,128)(2,1)S(1)}, bf16[6,6,24,384]{3,2,1,0:T(8,128)(2,1)}, u32[]{:S(2)}) copy-start(bf16[6,6,24,384]{3,2,1,0:T(8,128)(2,1)} %param.4) | copy-start | bytes 1990660
  177.4 6.8 %collective-permute-start.35 = (f32[9,1,25,128]{3,2,1,0:T(8,128)S(1)}, f32[9,1,25,128]{3,2,1,0:T(8,128)S(1)}, u32[]{:S(2)}, u32[]{:S(2)}) collective-permute-start(f32[9,1,25,128]{3,2,1,0:T(8,128)S(1)} %get-tuple-element.40), channel_id=1, source_target_pairs={{0,4},{4,0},{1,5},{5,1},{2,6},{6,2},{3,7},{7,3},{8,12},{12,8},{9,1... | collective-permute-start | bytes 345608 | tf_op jit(solution)/shard_map/ppermute | solution.py:24
  179.0 7.5 %collective-permute-start.36 = (f32[9,1,25,128]{3,2,1,0:T(8,128)S(1)}, f32[9,1,25,128]{3,2,1,0:T(8,128)S(1)}, u32[]{:S(2)}, u32[]{:S(2)}) collective-permute-start(f32[9,1,25,128]{3,2,1,0:T(8,128)S(1)} %get-tuple-element.41), channel_id=1, source_target_pairs={{4,0},{0,4},{5,1},{1,5},{6,2},{2,6},{7,3},{3,7},{12,8},{8,12},{13,... | collective-permute-start | bytes 345608 | tf_op jit(solution)/shard_map/ppermute | solution.py:26
  186.5 3.5 collective-permute-start.37
  186.6 3.6 %collective-permute-start.38 = (f32[9,9,1,128]{3,2,1,0:T(1,128)S(1)}, f32[9,9,1,128]{3,2,1,0:T(1,128)S(1)}, u32[]{:S(2)}, u32[]{:S(2)}) collective-permute-start(f32[9,9,1,128]{3,2,1,0:T(1,128)S(1)} %get-tuple-element.27), channel_id=1, source_target_pairs={{1,0},{2,1},{3,2},{0,3},{5,4},{6,5},{7,6},{4,7},{9,8},{10,9},{11,1... | collective-permute-start | bytes 124424 | tf_op jit(solution)/shard_map/ppermute | solution.py:26
  190.9 1.1 copy-start.4
  324.8 3.0 copy-start.2
  324.8 3.0 copy-start.5
Sparse Core Ops, SparseCore 0:
  194.3 130.4 all-reduce.56
where the time goes:
time: 367 us; the launch traced here: 360 us
  waiting for transfers between devices  217 us (59%)
  starting transfers between devices  54.2 us (15%)
  other arithmetic  37.1 us (10%)
  local copies, waits for them, and re-layouts  25.1 us (7%)
  between operations  15.6 us (4%)
  matrix products  11.5 us (3%)
    psum x1, waiting for transfers between devices, per_device(): lax.psum((cross_part, self_part, locked_part), ('gx', 'gy', 'gz'))  131 us
    ppermute x18, waiting for transfers between devices, padded_2(): lax.ppermute(tail, axis, [(i, (i + 1) % count) for i in range(count)])  57.8 us
    ppermute x18, starting transfers between devices, padded_2(): lax.ppermute(head, axis, [((i + 1) % count, i) for i in range(count)])  31.1 us
    ppermute x18, waiting for transfers between devices, padded_2(): lax.ppermute(head, axis, [((i + 1) % count, i) for i in range(count)])  23.6 us
    ppermute x18, starting transfers between devices, padded_2(): lax.ppermute(tail, axis, [(i, (i + 1) % count) for i in range(count)])  16.4 us
    another operation x3, other arithmetic, normalize(): factor = jnp.linalg.cholesky(gram_matrix)  12.4 us
    another operation x2, other arithmetic, normalize(): jax.scipy.linalg.solve_triangular(factor, jnp.eye(gram_matrix.shape[0], d...  10.5 us
    slice x6, local copies, waits for them, and re-layouts, split_cells(): lax.slice_in_dim(grown, ORDER, ORDER * cell_count + 1, stride=ORDER, axis...  8.9 us
  transfers between devices with their start and end apart: 40, of which 36 were waited for; matrix products, arithmetic and copies ran while one was open for 1% of the time, Pallas kernels for 0%

commit v1 on v0

v1 whole, which is shorter than its diff:
```python
import functools

import jax
import jax.numpy as jnp
import numpy as np
from jax import lax
from jax.experimental import pallas as pl
from jax.experimental.pallas import tpu as pltpu
from jax.sharding import PartitionSpec as P

ORDER = 6
SIDE = ORDER + 1
TILE = 8
LINES = SIDE * SIDE
CELL_ROWS = LINES * TILE
APPLY = 6
AXES = ("gx", "gy", "gz")

filter_low = 3.0
filter_high = 40.0
filter_bottom = 0.5

MESH = pl.DeviceIdType.MESH
HIGHEST = lax.Precision.HIGHEST

Z_STEPS = ((0, 0, 1), (0, 0, -1))
X_STEPS = ((1, 0, 0), (-1, 0, 0))
Y_STEPS = ((0, 1, 0), (0, -1, 0))
XY_STEPS = ((1, 1, 0), (1, -1, 0), (-1, 1, 0), (-1, -1, 0))


def recurrence():
    half = (filter_high - filter_low) / 2.0
    center = (filter_high + filter_low) / 2.0
    first = half / (filter_bottom - center)
    rows = [(first / half, center, 0.0)]
    now = first
    for _ in range(APPLY - 1):
        later = 1.0 / (2.0 / first - now)
        rows.append((2.0 * later / half, center, now * later))
        now = later
    return np.asarray(rows, np.float32)


def side_of(step):
    return ORDER if step > 0 else 0


def dot_rows(a, b, precision=None):
    return lax.dot_general(
        a, b, (((0,), (0,)), ((), ())), precision=precision, preferred_element_type=jnp.float32
    )


def groups(sizes, rows):
    for scattered in (("gy", "gz"), ("gz",)):
        count = int(np.prod([sizes[a] for a in scattered]))
        if rows % (16 * count) == 0:
            return scattered, tuple(a for a in AXES if a not in scattered)
    return (), AXES


def count_of(sizes, axes):
    return int(np.prod([sizes[a] for a in axes], dtype=np.int64))


def index_in(sizes, axes):
    index = 0
    for axis in axes:
        index = index * sizes[axis] + lax.axis_index(axis)
    return index


def device_at(sizes, axes, index):
    place = {axis: lax.axis_index(axis) for axis in AXES}
    for axis in reversed(axes):
        place[axis] = lax.rem(index, sizes[axis])
        index = index // sizes[axis]
    return tuple(place[axis] for axis in AXES)


def neighbour(sizes, step):
    return tuple(
        lax.rem(lax.axis_index(axis) + d + sizes[axis], sizes[axis]) for axis, d in zip(AXES, step)
    )


def greeted(sizes, all_axes):
    steps = {
        tuple(d % sizes[a] for a, d in zip(AXES, step))
        for step in Z_STEPS + X_STEPS + Y_STEPS + XY_STEPS
    }
    for axes in all_axes:
        for place in np.ndindex(*[sizes[a] for a in axes]):
            near = dict(zip(axes, place))
            steps.add(tuple(int(near.get(a, 0)) for a in AXES))
    steps.discard((0, 0, 0))
    return sorted(steps)


def exchange(sizes, axes, source, slots, send_sem, recv_sem):
    count = count_of(sizes, axes)
    me = index_in(sizes, axes)
    copies = []
    for r in range(1, count):
        place = lax.rem(me + r, count)
        copies.append(
            pltpu.make_async_remote_copy(
                src_ref=source(place),
                dst_ref=slots.at[me],
                send_sem=send_sem.at[r - 1],
                recv_sem=recv_sem.at[r - 1],
                device_id=device_at(sizes, axes, place),
                device_id_type=MESH,
            )
        )
    for copy in copies:
        copy.start()
    for copy in copies:
        copy.wait()


def sum_over_devices(sizes, part, scratch, finish, gathered):
    scattered, whole = groups(sizes, part.shape[0])
    if scattered:
        slots, send_sem, recv_sem = scratch[0]
        chunk = slots.shape[1]
        me = index_in(sizes, scattered)
        rows = lambda place: part.at[pl.ds(pl.multiple_of(place * chunk, chunk), chunk)]
        slots[me] = rows(me)[...]
        exchange(sizes, scattered, rows, slots, send_sem, recv_sem)
        total = jnp.sum(slots[...], axis=0)
    else:
        me = 0
        total = part[...]
    for axis, (slots, send_sem, recv_sem) in zip(whole, scratch[1:-1]):
        place = lax.axis_index(axis)
        slots[place] = total
        exchange(sizes, (axis,), lambda _: slots.at[place], slots, send_sem, recv_sem)
        total = jnp.sum(slots[...], axis=0)
    gathered[me] = finish(total)
    if scattered:
        send_sem, recv_sem = scratch[-1]
        exchange(sizes, scattered, lambda _: gathered.at[me], gathered, send_sem, recv_sem)


def sum_scratch(sizes, rows, width):
    scattered, whole = groups(sizes, rows)
    count = count_of(sizes, scattered)
    chunk = rows // count
    sems = lambda n: [pltpu.SemaphoreType.DMA((max(n - 1, 1),))] * 2
    shapes = [[pltpu.VMEM((count, chunk, width), jnp.float32)] + sems(count)]
    for axis in whole:
        n = sizes[axis]
        shapes.append([pltpu.VMEM((n, chunk, width), jnp.float32)] + sems(n))
    shapes.append(sems(count))
    return shapes


def halo_sum(sizes, slot, work, z_send, z_recv, f_send, f_recv, e_send, e_recv, sems, cells):
    send_sem, recv_sem = sems
    width = work.shape[1]

    def remote(number, step, source, target):
        return pltpu.make_async_remote_copy(
            src_ref=source,
            dst_ref=target,
            send_sem=send_sem.at[slot, number],
            recv_sem=recv_sem.at[slot, number],
            device_id=neighbour(sizes, step),
            device_id_type=MESH,
        )

    def z_rows(cell, c):
        return pl.ds(cell * CELL_ROWS + c, LINES, stride=TILE)

    top, bottom = z_rows(cells - 1, ORDER), z_rows(0, 0)
    z_send[slot, 0] = work[top, :]
    z_send[slot, 1] = work[bottom, :]
    z_copies = [
        remote(n, step, z_send.at[slot, n], z_recv.at[slot, n]) for n, step in enumerate(Z_STEPS)
    ]
    for copy in z_copies:
        copy.start()
    for cell in range(cells - 1):
        lower, upper = z_rows(cell, ORDER), z_rows(cell + 1, 0)
        both = work[lower, :] + work[upper, :]
        work[lower, :] = both
        work[upper, :] = both
    for copy in z_copies:
        copy.wait()
    work[bottom, :] = work[bottom, :] + z_recv[slot, 0]
    work[top, :] = work[top, :] + z_recv[slot, 1]

    def x_rows(cell, a):
        return pl.ds(cell * CELL_ROWS + a * SIDE * TILE, SIDE * TILE)

    def line(cell, a, b):
        return pl.ds(cell * CELL_ROWS + (a * SIDE + b) * TILE, TILE)

    copies = []
    number = len(Z_STEPS)
    for n, step in enumerate(X_STEPS):
        face = [work[x_rows(k, side_of(step[0])), :] for k in range(cells)]
        f_send[slot, n] = jnp.concatenate(face, 0).astype(f_send.dtype)
        copies.append(remote(number + n, step, f_send.at[slot, n], f_recv.at[slot, n]))
        copies[-1].start()
    for n, step in enumerate(Y_STEPS, len(X_STEPS)):
        b = side_of(step[1])
        face = [work[line(k, a, b), :] for k in range(cells) for a in range(SIDE)]
        f_send[slot, n] = jnp.concatenate(face, 0).astype(f_send.dtype)
        copies.append(remote(number + n, step, f_send.at[slot, n], f_recv.at[slot, n]))
        copies[-1].start()
    number += len(X_STEPS) + len(Y_STEPS)
    for n, step in enumerate(XY_STEPS):
        a, b = side_of(step[0]), side_of(step[1])
        edge = [work[line(k, a, b), :] for k in range(cells)]
        e_send[slot, n] = jnp.concatenate(edge, 0).astype(e_send.dtype)
        copies.append(remote(number + n, step, e_send.at[slot, n], e_recv.at[slot, n]))
        copies[-1].start()
    for copy in copies:
        copy.wait()
    for n, step in enumerate(X_STEPS):
        got = f_recv[slot, n].astype(jnp.float32).reshape(cells, SIDE * TILE, width)
        for k in range(cells):
            at = x_rows(k, side_of(-step[0]))
            work[at, :] = work[at, :] + got[k]
    for n, step in enumerate(Y_STEPS, len(X_STEPS)):
        got = f_recv[slot, n].astype(jnp.float32).reshape(cells, SIDE, TILE, width)
        for k in range(cells):
            for a in range(SIDE):
                at = line(k, a, side_of(-step[1]))
                work[at, :] = work[at, :] + got[k, a]
    for n, step in enumerate(XY_STEPS):
        got = e_recv[slot, n].astype(jnp.float32).reshape(cells, TILE, width)
        for k in range(cells):
            at = line(k, side_of(-step[0]), side_of(-step[1]))
            work[at, :] = work[at, :] + got[k]


def inverse_factor(gram, both, inverse):
    n = gram.shape[0]
    row = lax.broadcasted_iota(jnp.int32, (n, n), 0)
    col = lax.broadcasted_iota(jnp.int32, (n, n), 1)
    both[:, :n] = gram
    both[:, n:] = jnp.where(row == col, 1.0, 0.0).astype(jnp.float32)
    sub = lax.broadcasted_iota(jnp.int32, (TILE, n), 0)
    for start in range(0, n, TILE):
        left = both[start : start + TILE, :n]
        right = both[start : start + TILE, n:]
        cols = [
            jnp.broadcast_to(left[:, start + t : start + t + 1], (TILE, n)) for t in range(TILE)
        ]
        scale = jnp.zeros((TILE, n), jnp.float32)
        for s in range(TILE):
            pivot = jnp.broadcast_to(cols[s][s : s + 1, :], (TILE, n))
            scale = jnp.where(sub == s, lax.rsqrt(pivot), scale)
            if s + 1 < TILE:
                ratio = jnp.where(sub > s, cols[s] / pivot, 0.0)
                for t in range(s + 1, TILE):
                    cols[t] = cols[t] - ratio * cols[t][s : s + 1, :]
                left = left - ratio * left[s : s + 1, :]
                right = right - ratio * right[s : s + 1, :]
        left = left * scale
        right = right * scale
        inverse[start : start + TILE, :] = right
        if start + TILE < n:
            rows = jnp.concatenate([left, right], axis=1)
            both[...] = both[...] - dot_rows(left, rows, HIGHEST)


def kernel(
    sizes,
    cells,
    nodes_total,
    coef_ref,
    start_ref,
    locked_ref,
    h_ref,
    out_ref,
    padded_h,
    grid_nodes,
    state,
    work,
    z_send,
    z_recv,
    f_send,
    f_recv,
    e_send,
    e_recv,
    halo_sems,
    cross_part,
    cross_scratch,
    coefficient,
    gram_part,
    gram_scratch,
    gram_rows,
    both,
    inverse,
):
    width = work.shape[1]
    node = h_ref.shape[1]
    steps = greeted(sizes, [groups(sizes, locked_ref.shape[1])[0], groups(sizes, width)[0], *[(a,) for a in AXES]])
    barrier = pltpu.get_barrier_semaphore()
    for step in steps:
        pl.semaphore_signal(
            barrier, inc=1, device_id=neighbour(sizes, step), device_id_type=MESH
        )

    row = lax.broadcasted_iota(jnp.int32, (CELL_ROWS, node), 0)
    col = lax.broadcasted_iota(jnp.int32, (CELL_ROWS, node), 1)
    place = jnp.where(row % TILE < SIDE, row // TILE * SIDE + row % TILE, -1)
    spread = jnp.where(col == place, 1.0, 0.0).astype(jnp.bfloat16)
    for k in range(cells):
        tall = jnp.dot(spread, h_ref[k], preferred_element_type=jnp.float32).astype(jnp.bfloat16)
        padded_h[k] = lax.dot_general(
            tall, spread, (((1,), (1,)), ((), ())), preferred_element_type=jnp.float32
        ).astype(jnp.bfloat16)

    own = start_ref.shape[2]
    grid_nodes[...] = jnp.zeros_like(grid_nodes)
    grid_nodes[:, :, :own, :] = start_ref[...].astype(jnp.float32)
    work[...] = jnp.zeros_like(work)
    sub = lax.broadcasted_iota(jnp.int32, (ORDER, TILE, width), 1)
    for k in range(cells):
        for a in range(ORDER):
            values = grid_nodes[a, :, ORDER * k : ORDER * k + TILE, :]
            first = k * CELL_ROWS + a * SIDE * TILE
            work[first : first + ORDER * TILE, :] = jnp.where(sub < ORDER, values, 0.0).reshape(
                ORDER * TILE, width
            )
    pl.semaphore_wait(barrier, len(steps))
    halo = (work, z_send, z_recv, f_send, f_recv, e_send, e_recv, halo_sems, cells)
    halo_sum(sizes, 0, *halo)
    state[0] = work[...]
    state[1] = jnp.zeros(state.shape[1:], jnp.float32)

    def apply(t, carry):
        now, slot = lax.rem(t - 1, 2), lax.rem(t, 2)
        for k in range(cells):
            rows = pl.ds(k * CELL_ROWS, CELL_ROWS)
            values = state[now, rows, :].astype(jnp.bfloat16)
            work[rows, :] = jnp.dot(padded_h[k], values, preferred_element_type=jnp.float32)
        halo_sum(sizes, slot, *halo)
        scale, shift, back = coef_ref[t - 1, 0], coef_ref[t - 1, 1], coef_ref[t - 1, 2]
        for k in range(cells):
            rows = pl.ds(k * CELL_ROWS, CELL_ROWS)
            state[slot, rows, :] = (
                scale * (work[rows, :] - shift * state[now, rows, :]) - back * state[slot, rows, :]
            )
        return carry

    lax.fori_loop(1, APPLY + 1, apply, 0)
    last = APPLY % 2
    for k in range(cells):
        for a in range(ORDER):
            first = k * CELL_ROWS + a * SIDE * TILE
            grid_nodes[a, :, ORDER * k : ORDER * k + TILE, :] = state[
                last, first : first + ORDER * TILE, :
            ].reshape(ORDER, TILE, width)
    filtered = (
        grid_nodes[:, :, :own, :].reshape(ORDER * ORDER * own, width).astype(jnp.bfloat16)
    )
    cross_part[...] = dot_rows(locked_ref[...], filtered)
    sum_over_devices(
        sizes,
        cross_part,
        cross_scratch,
        lambda total: (total / nodes_total).astype(jnp.bfloat16),
        coefficient,
    )
    projected = filtered.astype(jnp.float32) - jnp.dot(
        locked_ref[...],
        coefficient[...].reshape(locked_ref.shape[1], width),
        preferred_element_type=jnp.float32,
    )
    out_ref[...] = projected
    gram_part[...] = dot_rows(projected, projected, HIGHEST)
    sum_over_devices(sizes, gram_part, gram_scratch, lambda total: total / nodes_total, gram_rows)
    inverse_factor(gram_rows[...].reshape(width, width), both, inverse)
    out_ref[...] = lax.dot_general(
        out_ref[...],
        inverse[...],
        (((1,), (1,)), ((), ())),
        precision=HIGHEST,
        preferred_element_type=jnp.float32,
    )


def per_device(sizes, start_block, locked_orbitals, cell_h):
    width = start_block.shape[3]
    locked = locked_orbitals.shape[3]
    own = start_block.shape[2]
    cells = cell_h.shape[2]
    assert cell_h.shape[:2] == (1, 1)
    nodes = ORDER * ORDER * own
    nodes_total = float(nodes * count_of(sizes, AXES))
    count = lambda rows: count_of(sizes, groups(sizes, rows)[0])
    face = cells * SIDE * TILE
    messages = len(Z_STEPS) + len(X_STEPS) + len(Y_STEPS) + len(XY_STEPS)
    vmem = pltpu.VMEM
    scratch = [
        vmem((cells, CELL_ROWS, CELL_ROWS), jnp.bfloat16),
        vmem((ORDER, ORDER, own + TILE, width), jnp.float32),
        vmem((2, cells * CELL_ROWS, width), jnp.float32),
        vmem((cells * CELL_ROWS, width), jnp.float32),
        vmem((2, 2, LINES, width), jnp.float32),
        vmem((2, 2, LINES, width), jnp.float32),
        vmem((2, 4, face, width), jnp.bfloat16),
        vmem((2, 4, face, width), jnp.bfloat16),
        vmem((2, 4, cells * TILE, width), jnp.bfloat16),
        vmem((2, 4, cells * TILE, width), jnp.bfloat16),
        [pltpu.SemaphoreType.DMA((2, messages))] * 2,
        vmem((locked, width), jnp.float32),
        sum_scratch(sizes, locked, width),
        vmem((count(locked), locked // count(locked), width), jnp.bfloat16),
        vmem((width, width), jnp.float32),
        sum_scratch(sizes, width, width),
        vmem((count(width), width // count(width), width), jnp.float32),
        vmem((width, 2 * width), jnp.float32),
        vmem((width, width), jnp.float32),
    ]
    result = pl.pallas_call(
        functools.partial(kernel, sizes, cells, nodes_total),
        out_shape=jax.ShapeDtypeStruct((nodes, width), jnp.float32),
        in_specs=[pl.BlockSpec(memory_space=pltpu.SMEM)]
        + [pl.BlockSpec(memory_space=pltpu.VMEM)] * 3,
        out_specs=pl.BlockSpec(memory_space=pltpu.VMEM),
        scratch_shapes=scratch,
        compiler_params=pltpu.CompilerParams(
            collective_id=0, has_side_effects=True, vmem_limit_bytes=40 << 20
        ),
    )(
        jnp.asarray(recurrence()),
        start_block,
        locked_orbitals.reshape(nodes, locked),
        cell_h.reshape(cell_h.shape[2:]),
    )
    return result.reshape(start_block.shape)


def solution(mesh):
    sizes = dict(mesh.shape)
    placed = (P("gx", "gy", "gz", None), P("gx", "gy", "gz", None), P("gx", "gy", "gz", None, None))
    return jax.shard_map(
        functools.partial(per_device, sizes),
        mesh=mesh,
        in_specs=placed,
        out_specs=P("gx", "gy", "gz", None),
        check_vma=False,
    )
```

time: 367 us -> 110 us (0.30); the launches traced: 360 us -> 110 us
  waiting for transfers between devices: 217 us -> 0 us
  Pallas kernels: 0 us -> 108 us
  starting transfers between devices: 54.2 us -> 0 us
  other arithmetic: 37.1 us -> 0 us
  local copies, waits for them, and re-layouts: 25.1 us -> 2.22 us
  between operations: 15.6 us -> 0.04 us
  matrix products: 11.5 us -> 0 us
    psum x1 -> x0, waiting for transfers between devices: 131 us -> none  [per_device(): lax.psum((cross_part, self_part, locked_part), ('gx', 'gy', 'gz'))]
    pallas_call x0 -> x1, Pallas kernels: none -> 108 us  [per_device(): pl.pallas_call(functools.partial(kernel, sizes, cells, nodes_total), out_...]
    ppermute x39 -> x0, waiting for transfers between devices: 86.2 us -> none  [the longest x18 57.8 us: padded_2(): lax.ppermute(tail, axis, [(i, (i + 1) % count) for i in range(count)])]
    ppermute x39 -> x0, starting transfers between devices: 54.2 us -> none  [the longest x18 31.1 us: padded_2(): lax.ppermute(head, axis, [((i + 1) % count, i) for i in range(count)])]
    another operation x6 -> x0, other arithmetic: 23 us -> none  [the longest x3 12.4 us: normalize(): factor = jnp.linalg.cholesky(gram_matrix)]
    slice x50 -> x0, local copies, waits for them, and re-layouts: 16.2 us -> none  [the longest x6 8.9 us: split_cells(): lax.slice_in_dim(grown, ORDER, ORDER * cell_count + 1, stride=ORDER, axis...]
    dot_general x14 -> x0, matrix products: 11.3 us -> none  [the longest x6 3.09 us: cell_terms(): jnp.einsum('abcij,abcjv->abciv', cell_h, cell_local, preferred_element_ty...]
    concatenate x32 -> x0, other arithmetic: 5.09 us -> none  [the longest x12 2.72 us: split_cells(): return jnp.concatenate([head_part, tail_part], axis_pos + 1)]
  transfers between devices with their start and end apart: 40 -> 0, of which waited for: 36 -> 0; matrix products, arithmetic and copies ran while one was open for 1% -> 0% of each run, Pallas kernels for 0% -> 0%
where the time goes in v1:
time: 110 us
  Pallas kernels  108 us (98%)
  local copies, waits for them, and re-layouts  2.22 us (2%)
    pallas_call x1, Pallas kernels, per_device(): pl.pallas_call(functools.partial(kernel, sizes, cells, nodes_total), out_...  108 us
    unnamed x8, local copies, waits for them, and re-layouts  2.22 us

profile of v1, /device:TPU:0, one launch (start us, length us, event | category | flops | bytes accessed | tf_op | source)
XLA Modules:
  0.0 110.0 jit_solution(6494601992761642225)
XLA Ops:
  0.0 0.0 copy-start.2
  0.0 0.0 copy-start
  0.0 0.0 copy-start.1
  0.0 1.4 %copy.7 = bf16[1,1,4,343,343]{4,3,2,1,0:T(8,128)(2,1)S(1)} copy(bf16[1,1,4,343,343]{4,2,3,1,0:T(4,128)(2,1)} %param.6) | data formatting | bytes 1882384 | tf_op args[2]
  1.5 0.0 copy-done.2
  1.5 0.0 copy-done
  1.5 0.0 copy-done.1
  1.5 107.7 %shard_map.46 = f32[864,128]{1,0:T(8,128)S(1)} custom-call(f32[6,3]{1,0:T(8,128)S(1)} %copy-done.2, bf16[6,6,24,128]{3,2,1,0:T(8,128)(2,1)S(1)} %copy-done.1, bf16[864,384]{1,0:T(8,128)(2,1)S(1)} %bitcast.7, bf16[4,343,343]{2,1,0:T(8,128)(2,1)S(1)} %bitcast.5), custom_call_target="tpu_custom_call" | custom-call | tf_op jit(solution)/shard_map/pallas_call | solution.py:423
  109.2 0.8 copy.9
Async XLA Ops:
  0.0 1.5 %copy-start.2 = (f32[6,3]{1,0:T(8,128)S(1)}, f32[6,3]{1,0:T(8,128)}, u32[]{:S(2)}) copy-start(f32[6,3]{1,0:T(8,128)} %constant.2.clone.coef_ref) | copy-start | bytes 220
  0.0 1.5 %copy-start = (bf16[6,6,24,384]{3,2,1,0:T(8,128)(2,1)S(1)}, bf16[6,6,24,384]{3,2,1,0:T(8,128)(2,1)}, u32[]{:S(2)}) copy-start(bf16[6,6,24,384]{3,2,1,0:T(8,128)(2,1)} %param.5) | copy-start | bytes 1990660
  0.0 1.5 %copy-start.1 = (bf16[6,6,24,128]{3,2,1,0:T(8,128)(2,1)S(1)}, bf16[6,6,24,128]{3,2,1,0:T(8,128)(2,1)}, u32[]{:S(2)}) copy-start(bf16[6,6,24,128]{3,2,1,0:T(8,128)(2,1)} %start_ref.1) | copy-start | bytes 663556

commit v2 on v1

--- a/solution.py
+++ b/solution.py
@@ -14,6 +14,7 @@
 LINES = SIDE * SIDE
 CELL_ROWS = LINES * TILE
 APPLY = 6
+BLOCK_ROWS = 16
 AXES = ("gx", "gy", "gz")
 
 filter_low = 3.0
@@ -33,7 +34,7 @@
     half = (filter_high - filter_low) / 2.0
     center = (filter_high + filter_low) / 2.0
     first = half / (filter_bottom - center)
-    rows = [(first / half, center, 0.0)]
+    rows = [(1.0, 0.0, 0.0), (first / half, center, 0.0)]
     now = first
     for _ in range(APPLY - 1):
         later = 1.0 / (2.0 / first - now)
@@ -157,116 +158,142 @@
     return shapes
 
 
-def halo_sum(sizes, slot, work, z_send, z_recv, f_send, f_recv, e_send, e_recv, sems, cells):
-    send_sem, recv_sem = sems
-    width = work.shape[1]
-
-    def remote(number, step, source, target):
+def merged(sizes):
+    found = {}
+    for step in X_STEPS + Y_STEPS + XY_STEPS:
+        found.setdefault(tuple(d % sizes[a] for a, d in zip(AXES, step)), []).append(step)
+    return list(found.values())
+
+
+def part_rows(step, count):
+    return count * TILE * (SIDE if 0 in step[:2] else 1)
+
+
+class Halo:
+    def __init__(self, sizes, cells, work, z_send, z_recv, f_send, f_recv, sems):
+        self.sizes, self.cells, self.work = sizes, cells, work
+        self.z_send, self.z_recv = z_send, z_recv
+        self.f_send, self.f_recv = f_send, f_recv
+        self.send_sem, self.recv_sem = sems
+        self.messages = merged(sizes)
+
+    def remote(self, slot, number, step, source, target):
         return pltpu.make_async_remote_copy(
             src_ref=source,
             dst_ref=target,
-            send_sem=send_sem.at[slot, number],
-            recv_sem=recv_sem.at[slot, number],
-            device_id=neighbour(sizes, step),
+            send_sem=self.send_sem.at[slot, number],
+            recv_sem=self.recv_sem.at[slot, number],
+            device_id=neighbour(self.sizes, step),
             device_id_type=MESH,
         )
 
-    def z_rows(cell, c):
+    def lines(self, cell, step):
+        first = cell * CELL_ROWS
+        if step[1] == 0:
+            return [pl.ds(first + side_of(step[0]) * SIDE * TILE, SIDE * TILE)]
+        if step[0] == 0:
+            rows = range(SIDE)
+        else:
+            rows = [side_of(step[0])]
+        return [pl.ds(first + (a * SIDE + side_of(step[1])) * TILE, TILE) for a in rows]
+
+    def send_faces(self, slot, group, cells):
+        copies = []
+        row = 0
+        for n, steps in enumerate(self.messages):
+            begin = row
+            for step in steps:
+                part = [self.work[at, :] for k in cells for at in self.lines(k, step)]
+                size = part_rows(step, len(cells))
+                self.f_send[slot, group, row : row + size, :] = jnp.concatenate(part, 0).astype(
+                    self.f_send.dtype
+                )
+                row += size
+            rows = pl.ds(begin, row - begin)
+            copies.append(
+                self.remote(
+                    slot,
+                    len(Z_STEPS) + group * len(self.messages) + n,
+                    steps[0],
+                    self.f_send.at[slot, group, rows],
+                    self.f_recv.at[slot, group, rows],
+                )
+            )
+            copies[-1].start()
+        return copies
+
+    def add_faces(self, slot, group, cells, copies):
+        row = 0
+        for copy, steps in zip(copies, self.messages):
+            copy.wait()
+            for step in steps:
+                size = part_rows(step, len(cells))
+                got = self.f_recv[slot, group, row : row + size, :].astype(jnp.float32)
+                row += size
+                taken = 0
+                for k in cells:
+                    for at in self.lines(k, tuple(-d for d in step)):
+                        self.work[at, :] = self.work[at, :] + got[taken : taken + at.size]
+                        taken += at.size
+
+    def z_rows(self, cell, c):
         return pl.ds(cell * CELL_ROWS + c, LINES, stride=TILE)
 
-    top, bottom = z_rows(cells - 1, ORDER), z_rows(0, 0)
-    z_send[slot, 0] = work[top, :]
-    z_send[slot, 1] = work[bottom, :]
-    z_copies = [
-        remote(n, step, z_send.at[slot, n], z_recv.at[slot, n]) for n, step in enumerate(Z_STEPS)
-    ]
-    for copy in z_copies:
-        copy.start()
-    for cell in range(cells - 1):
-        lower, upper = z_rows(cell, ORDER), z_rows(cell + 1, 0)
-        both = work[lower, :] + work[upper, :]
-        work[lower, :] = both
-        work[upper, :] = both
-    for copy in z_copies:
-        copy.wait()
-    work[bottom, :] = work[bottom, :] + z_recv[slot, 0]
-    work[top, :] = work[top, :] + z_recv[slot, 1]
-
-    def x_rows(cell, a):
-        return pl.ds(cell * CELL_ROWS + a * SIDE * TILE, SIDE * TILE)
-
-    def line(cell, a, b):
-        return pl.ds(cell * CELL_ROWS + (a * SIDE + b) * TILE, TILE)
-
-    copies = []
-    number = len(Z_STEPS)
-    for n, step in enumerate(X_STEPS):
-        face = [work[x_rows(k, side_of(step[0])), :] for k in range(cells)]
-        f_send[slot, n] = jnp.concatenate(face, 0).astype(f_send.dtype)
-        copies.append(remote(number + n, step, f_send.at[slot, n], f_recv.at[slot, n]))
-        copies[-1].start()
-    for n, step in enumerate(Y_STEPS, len(X_STEPS)):
-        b = side_of(step[1])
-        face = [work[line(k, a, b), :] for k in range(cells) for a in range(SIDE)]
-        f_send[slot, n] = jnp.concatenate(face, 0).astype(f_send.dtype)
-        copies.append(remote(number + n, step, f_send.at[slot, n], f_recv.at[slot, n]))
-        copies[-1].start()
-    number += len(X_STEPS) + len(Y_STEPS)
-    for n, step in enumerate(XY_STEPS):
-        a, b = side_of(step[0]), side_of(step[1])
-        edge = [work[line(k, a, b), :] for k in range(cells)]
-        e_send[slot, n] = jnp.concatenate(edge, 0).astype(e_send.dtype)
-        copies.append(remote(number + n, step, e_send.at[slot, n], e_recv.at[slot, n]))
-        copies[-1].start()
-    for copy in copies:
-        copy.wait()
-    for n, step in enumerate(X_STEPS):
-        got = f_recv[slot, n].astype(jnp.float32).reshape(cells, SIDE * TILE, width)
-        for k in range(cells):
-            at = x_rows(k, side_of(-step[0]))
-            work[at, :] = work[at, :] + got[k]
-    for n, step in enumerate(Y_STEPS, len(X_STEPS)):
-        got = f_recv[slot, n].astype(jnp.float32).reshape(cells, SIDE, TILE, width)
-        for k in range(cells):
-            for a in range(SIDE):
-                at = line(k, a, side_of(-step[1]))
-                work[at, :] = work[at, :] + got[k, a]
-    for n, step in enumerate(XY_STEPS):
-        got = e_recv[slot, n].astype(jnp.float32).reshape(cells, TILE, width)
-        for k in range(cells):
-            at = line(k, side_of(-step[0]), side_of(-step[1]))
-            work[at, :] = work[at, :] + got[k]
-
-
-def inverse_factor(gram, both, inverse):
+    def z_copies(self, slot):
+        return [
+            self.remote(slot, n, step, self.z_send.at[slot, n], self.z_recv.at[slot, n])
+            for n, step in enumerate(Z_STEPS)
+        ]
+
+    def send_z(self, slot):
+        work = self.work
+        self.z_send[slot, 0] = work[self.z_rows(self.cells - 1, ORDER), :]
+        self.z_send[slot, 1] = work[self.z_rows(0, 0), :]
+        for copy in self.z_copies(slot):
+            copy.start()
+        for cell in range(self.cells - 1):
+            lower, upper = self.z_rows(cell, ORDER), self.z_rows(cell + 1, 0)
+            both = work[lower, :] + work[upper, :]
+            work[lower, :] = both
+            work[upper, :] = both
+
+    def add_z(self, slot):
+        work = self.work
+        for copy in self.z_copies(slot):
+            copy.wait()
+        bottom, top = self.z_rows(0, 0), self.z_rows(self.cells - 1, ORDER)
+        work[bottom, :] = work[bottom, :] + self.z_recv[slot, 0]
+        work[top, :] = work[top, :] + self.z_recv[slot, 1]
+
+
+def inverse_factor(gram, mixed, inverse):
     n = gram.shape[0]
-    row = lax.broadcasted_iota(jnp.int32, (n, n), 0)
-    col = lax.broadcasted_iota(jnp.int32, (n, n), 1)
-    both[:, :n] = gram
-    both[:, n:] = jnp.where(row == col, 1.0, 0.0).astype(jnp.float32)
-    sub = lax.broadcasted_iota(jnp.int32, (TILE, n), 0)
-    for start in range(0, n, TILE):
-        left = both[start : start + TILE, :n]
-        right = both[start : start + TILE, n:]
-        cols = [
-            jnp.broadcast_to(left[:, start + t : start + t + 1], (TILE, n)) for t in range(TILE)
-        ]
-        scale = jnp.zeros((TILE, n), jnp.float32)
-        for s in range(TILE):
-            pivot = jnp.broadcast_to(cols[s][s : s + 1, :], (TILE, n))
-            scale = jnp.where(sub == s, lax.rsqrt(pivot), scale)
-            if s + 1 < TILE:
-                ratio = jnp.where(sub > s, cols[s] / pivot, 0.0)
-                for t in range(s + 1, TILE):
+    size = BLOCK_ROWS if n % BLOCK_ROWS == 0 else TILE
+    mixed[...] = gram
+    sub = lax.broadcasted_iota(jnp.int32, (size, n), 0)
+    col = lax.broadcasted_iota(jnp.int32, (size, n), 1)
+    for start in range(0, n, size):
+        end = start + size
+        rows = mixed[start:end, :]
+        cols = [jnp.broadcast_to(rows[:, start + t : start + t + 1], (size, n)) for t in range(size)]
+        unit = jnp.where(col - start == sub, 1.0, 0.0).astype(jnp.float32)
+        rows = jnp.where((col >= start) & (col < end), unit, rows)
+        scale = jnp.zeros((size, n), jnp.float32)
+        for s in range(size):
+            root = lax.rsqrt(cols[s][s : s + 1, :])
+            scale = jnp.where(sub == s, root, scale)
+            if s + 1 < size:
+                ratio = jnp.where(sub > s, cols[s] * (root * root), 0.0)
+                for t in range(s + 1, size):
                     cols[t] = cols[t] - ratio * cols[t][s : s + 1, :]
-                left = left - ratio * left[s : s + 1, :]
-                right = right - ratio * right[s : s + 1, :]
-        left = left * scale
-        right = right * scale
-        inverse[start : start + TILE, :] = right
-        if start + TILE < n:
-            rows = jnp.concatenate([left, right], axis=1)
-            both[...] = both[...] - dot_rows(left, rows, HIGHEST)
+                rows = rows - ratio * rows[s : s + 1, :]
+        rows = rows * scale
+        inverse[start:end, :] = jnp.where(col < end, rows, 0.0)
+        if end < n:
+            change = dot_rows(jnp.where(col >= end, rows, 0.0), rows, HIGHEST)[end:, :]
+            rest = lax.broadcasted_iota(jnp.int32, (n - end, n), 1)
+            kept = jnp.where((rest >= start) & (rest < end), 0.0, mixed[end:, :])
+            mixed[end:, :] = kept - change
 
 
 def kernel(
@@ -286,8 +313,6 @@
     z_recv,
     f_send,
     f_recv,
-    e_send,
-    e_recv,
     halo_sems,
     cross_part,
     cross_scratch,
@@ -295,7 +320,7 @@
     gram_part,
     gram_scratch,
     gram_rows,
-    both,
+    mixed,
     inverse,
 ):
     width = work.shape[1]
@@ -330,27 +355,48 @@
                 ORDER * TILE, width
             )
     pl.semaphore_wait(barrier, len(steps))
-    halo = (work, z_send, z_recv, f_send, f_recv, e_send, e_recv, halo_sems, cells)
-    halo_sum(sizes, 0, *halo)
-    state[0] = work[...]
-    state[1] = jnp.zeros(state.shape[1:], jnp.float32)
+    halo = Halo(sizes, cells, work, z_send, z_recv, f_send, f_recv, halo_sems)
+    inner, outer = tuple(range(1, cells - 1)), (0, cells - 1)
+    state[...] = jnp.zeros(state.shape, jnp.float32)
+
+    def finish_faces(slot, inner_copies, outer_copies):
+        halo.add_faces(slot, 0, inner, inner_copies)
+        halo.add_faces(slot, 1, outer, outer_copies)
+        halo.send_z(slot)
+
+    def update(t, group):
+        now, old = lax.rem(t, 2), lax.rem(t + 1, 2)
+        scale, shift, back = coef_ref[t, 0], coef_ref[t, 1], coef_ref[t, 2]
+        for k in group:
+            rows = pl.ds(k * CELL_ROWS, CELL_ROWS)
+            state[now, rows, :] = (
+                scale * (work[rows, :] - shift * state[old, rows, :]) - back * state[now, rows, :]
+            )
+
+    def multiply(t, group):
+        for k in group:
+            rows = pl.ds(k * CELL_ROWS, CELL_ROWS)
+            values = state[lax.rem(t, 2), rows, :].astype(jnp.bfloat16)
+            work[rows, :] = jnp.dot(padded_h[k], values, preferred_element_type=jnp.float32)
+
+    finish_faces(0, halo.send_faces(0, 0, inner), halo.send_faces(0, 1, outer))
 
     def apply(t, carry):
-        now, slot = lax.rem(t - 1, 2), lax.rem(t, 2)
-        for k in range(cells):
-            rows = pl.ds(k * CELL_ROWS, CELL_ROWS)
-            values = state[now, rows, :].astype(jnp.bfloat16)
-            work[rows, :] = jnp.dot(padded_h[k], values, preferred_element_type=jnp.float32)
-        halo_sum(sizes, slot, *halo)
-        scale, shift, back = coef_ref[t - 1, 0], coef_ref[t - 1, 1], coef_ref[t - 1, 2]
-        for k in range(cells):
-            rows = pl.ds(k * CELL_ROWS, CELL_ROWS)
-            state[slot, rows, :] = (
-                scale * (work[rows, :] - shift * state[now, rows, :]) - back * state[slot, rows, :]
-            )
+        slot = lax.rem(t, 2)
+        update(t - 1, inner)
+        multiply(t - 1, inner)
+        inner_copies = halo.send_faces(slot, 0, inner)
+        halo.add_z(lax.rem(t - 1, 2))
+        update(t - 1, outer)
+        multiply(t - 1, outer)
+        outer_copies = halo.send_faces(slot, 1, outer)
+        finish_faces(slot, inner_copies, outer_copies)
         return carry
 
     lax.fori_loop(1, APPLY + 1, apply, 0)
+    update(APPLY, inner)
+    halo.add_z(APPLY % 2)
+    update(APPLY, outer)
     last = APPLY % 2
     for k in range(cells):
         for a in range(ORDER):
@@ -377,7 +423,7 @@
     out_ref[...] = projected
     gram_part[...] = dot_rows(projected, projected, HIGHEST)
     sum_over_devices(sizes, gram_part, gram_scratch, lambda total: total / nodes_total, gram_rows)
-    inverse_factor(gram_rows[...].reshape(width, width), both, inverse)
+    inverse_factor(gram_rows[...].reshape(width, width), mixed, inverse)
     out_ref[...] = lax.dot_general(
         out_ref[...],
         inverse[...],
@@ -396,8 +442,9 @@
     nodes = ORDER * ORDER * own
     nodes_total = float(nodes * count_of(sizes, AXES))
     count = lambda rows: count_of(sizes, groups(sizes, rows)[0])
-    face = cells * SIDE * TILE
-    messages = len(Z_STEPS) + len(X_STEPS) + len(Y_STEPS) + len(XY_STEPS)
+    largest = max(cells - 2, 2)
+    faces = sum(part_rows(step, largest) for step in X_STEPS + Y_STEPS + XY_STEPS)
+    messages = len(Z_STEPS) + 2 * len(merged(sizes))
     vmem = pltpu.VMEM
     scratch = [
         vmem((cells, CELL_ROWS, CELL_ROWS), jnp.bfloat16),
@@ -406,10 +453,8 @@
         vmem((cells * CELL_ROWS, width), jnp.float32),
         vmem((2, 2, LINES, width), jnp.float32),
         vmem((2, 2, LINES, width), jnp.float32),
-        vmem((2, 4, face, width), jnp.bfloat16),
-        vmem((2, 4, face, width), jnp.bfloat16),
-        vmem((2, 4, cells * TILE, width), jnp.bfloat16),
-        vmem((2, 4, cells * TILE, width), jnp.bfloat16),
+        vmem((2, 2, faces, width), jnp.bfloat16),
+        vmem((2, 2, faces, width), jnp.bfloat16),
         [pltpu.SemaphoreType.DMA((2, messages))] * 2,
         vmem((locked, width), jnp.float32),
         sum_scratch(sizes, locked, width),
@@ -417,7 +462,7 @@
         vmem((width, width), jnp.float32),
         sum_scratch(sizes, width, width),
         vmem((count(width), width // count(width), width), jnp.float32),
-        vmem((width, 2 * width), jnp.float32),
+        vmem((width, width), jnp.float32),
         vmem((width, width), jnp.float32),
     ]
     result = pl.pallas_call(

time: 110 us -> 94.9 us (0.86)
  Pallas kernels: 108 us -> 92.5 us
    pallas_call x1, Pallas kernels: 108 us -> 92.5 us  [per_device(): pl.pallas_call(functools.partial(kernel, sizes, cells, nodes_total), out_...]
where the time goes in v2:
time: 94.9 us; the launch traced here: 94.8 us
  Pallas kernels  92.5 us (97%)
  local copies, waits for them, and re-layouts  2.22 us (2%)
    pallas_call x1, Pallas kernels, per_device(): pl.pallas_call(functools.partial(kernel, sizes, cells, nodes_total), out_...  92.5 us
    unnamed x8, local copies, waits for them, and re-layouts  2.22 us

profile of v2, /device:TPU:0, one launch (start us, length us, event | category | flops | bytes accessed | tf_op | source)
XLA Modules:
  0.0 94.8 jit_solution(12323582315555020127)
XLA Ops:
  0.0 0.0 copy-start.2
  0.0 0.0 copy-start
  0.0 0.0 copy-start.1
  0.0 1.4 %copy.7 = bf16[1,1,4,343,343]{4,3,2,1,0:T(8,128)(2,1)S(1)} copy(bf16[1,1,4,343,343]{4,2,3,1,0:T(4,128)(2,1)} %param.6) | data formatting | bytes 1882384 | tf_op args[2]
  1.5 0.0 copy-done.2
  1.5 0.0 copy-done
  1.5 0.0 copy-done.1
  1.5 92.5 %shard_map.46 = f32[864,128]{1,0:T(8,128)S(1)} custom-call(f32[7,3]{1,0:T(8,128)S(1)} %copy-done.2, bf16[6,6,24,128]{3,2,1,0:T(8,128)(2,1)S(1)} %copy-done.1, bf16[864,384]{1,0:T(8,128)(2,1)S(1)} %bitcast.7, bf16[4,343,343]{2,1,0:T(8,128)(2,1)S(1)} %bitcast.5), custom_call_target="tpu_custom_call" | custom-call | tf_op jit(solution)/shard_map/pallas_call | solution.py:468
  94.0 0.8 copy.9
Async XLA Ops:
  0.0 1.5 %copy-start.2 = (f32[7,3]{1,0:T(8,128)S(1)}, f32[7,3]{1,0:T(8,128)}, u32[]{:S(2)}) copy-start(f32[7,3]{1,0:T(8,128)} %constant.2.clone.coef_ref) | copy-start | bytes 256
  0.0 1.5 %copy-start = (bf16[6,6,24,384]{3,2,1,0:T(8,128)(2,1)S(1)}, bf16[6,6,24,384]{3,2,1,0:T(8,128)(2,1)}, u32[]{:S(2)}) copy-start(bf16[6,6,24,384]{3,2,1,0:T(8,128)(2,1)} %param.5) | copy-start | bytes 1990660
  0.0 1.5 %copy-start.1 = (bf16[6,6,24,128]{3,2,1,0:T(8,128)(2,1)S(1)}, bf16[6,6,24,128]{3,2,1,0:T(8,128)(2,1)}, u32[]{:S(2)}) copy-start(bf16[6,6,24,128]{3,2,1,0:T(8,128)(2,1)} %start_ref.1) | copy-start | bytes 663556

commit v3 on v2

--- a/solution.py
+++ b/solution.py
@@ -51,6 +51,11 @@
     return lax.dot_general(
         a, b, (((0,), (0,)), ((), ())), precision=precision, preferred_element_type=jnp.float32
     )
+
+
+def split(values):
+    high = values.astype(jnp.bfloat16)
+    return high, (values - high.astype(jnp.float32)).astype(jnp.bfloat16)
 
 
 def groups(sizes, rows):
@@ -176,6 +181,8 @@
         self.f_send, self.f_recv = f_send, f_recv
         self.send_sem, self.recv_sem = sems
         self.messages = merged(sizes)
+        steps = Z_STEPS + tuple(steps[0] for steps in self.messages)
+        self.places = {step: neighbour(sizes, step) for step in steps}
 
     def remote(self, slot, number, step, source, target):
         return pltpu.make_async_remote_copy(
@@ -183,7 +190,7 @@
             dst_ref=target,
             send_sem=self.send_sem.at[slot, number],
             recv_sem=self.recv_sem.at[slot, number],
-            device_id=neighbour(self.sizes, step),
+            device_id=self.places[step],
             device_id_type=MESH,
         )
 
@@ -314,12 +321,14 @@
     f_send,
     f_recv,
     halo_sems,
+    locked_t,
     cross_part,
     cross_scratch,
     coefficient,
     gram_part,
     gram_scratch,
     gram_rows,
+    parts,
     mixed,
     inverse,
 ):
@@ -331,16 +340,6 @@
         pl.semaphore_signal(
             barrier, inc=1, device_id=neighbour(sizes, step), device_id_type=MESH
         )
-
-    row = lax.broadcasted_iota(jnp.int32, (CELL_ROWS, node), 0)
-    col = lax.broadcasted_iota(jnp.int32, (CELL_ROWS, node), 1)
-    place = jnp.where(row % TILE < SIDE, row // TILE * SIDE + row % TILE, -1)
-    spread = jnp.where(col == place, 1.0, 0.0).astype(jnp.bfloat16)
-    for k in range(cells):
-        tall = jnp.dot(spread, h_ref[k], preferred_element_type=jnp.float32).astype(jnp.bfloat16)
-        padded_h[k] = lax.dot_general(
-            tall, spread, (((1,), (1,)), ((), ())), preferred_element_type=jnp.float32
-        ).astype(jnp.bfloat16)
 
     own = start_ref.shape[2]
     grid_nodes[...] = jnp.zeros_like(grid_nodes)
@@ -379,7 +378,19 @@
             values = state[lax.rem(t, 2), rows, :].astype(jnp.bfloat16)
             work[rows, :] = jnp.dot(padded_h[k], values, preferred_element_type=jnp.float32)
 
-    finish_faces(0, halo.send_faces(0, 0, inner), halo.send_faces(0, 1, outer))
+    inner_copies = halo.send_faces(0, 0, inner)
+    outer_copies = halo.send_faces(0, 1, outer)
+    row = lax.broadcasted_iota(jnp.int32, (CELL_ROWS, node), 0)
+    col = lax.broadcasted_iota(jnp.int32, (CELL_ROWS, node), 1)
+    place = jnp.where(row % TILE < SIDE, row // TILE * SIDE + row % TILE, -1)
+    spread = jnp.where(col == place, 1.0, 0.0).astype(jnp.bfloat16)
+    for k in range(cells):
+        tall = jnp.dot(spread, h_ref[k], preferred_element_type=jnp.float32).astype(jnp.bfloat16)
+        padded_h[k] = lax.dot_general(
+            tall, spread, (((1,), (1,)), ((), ())), preferred_element_type=jnp.float32
+        ).astype(jnp.bfloat16)
+    locked_t[...] = locked_ref[...].T
+    finish_faces(0, inner_copies, outer_copies)
 
     def apply(t, carry):
         slot = lax.rem(t, 2)
@@ -407,7 +418,7 @@
     filtered = (
         grid_nodes[:, :, :own, :].reshape(ORDER * ORDER * own, width).astype(jnp.bfloat16)
     )
-    cross_part[...] = dot_rows(locked_ref[...], filtered)
+    cross_part[...] = jnp.dot(locked_t[...], filtered, preferred_element_type=jnp.float32)
     sum_over_devices(
         sizes,
         cross_part,
@@ -420,16 +431,24 @@
         coefficient[...].reshape(locked_ref.shape[1], width),
         preferred_element_type=jnp.float32,
     )
-    out_ref[...] = projected
-    gram_part[...] = dot_rows(projected, projected, HIGHEST)
+    high, low = split(projected)
+    parts[:, :width] = high
+    parts[:, width:] = low
+    terms = dot_rows(parts[...], parts[...])
+    gram_part[...] = (
+        terms[:width, :width]
+        + (terms[:width, width:] + terms[width:, :width])
+        + terms[width:, width:]
+    )
     sum_over_devices(sizes, gram_part, gram_scratch, lambda total: total / nodes_total, gram_rows)
     inverse_factor(gram_rows[...].reshape(width, width), mixed, inverse)
+    inverse_high, inverse_low = split(inverse[...])
+    wide = jnp.concatenate([inverse_high, inverse_high], axis=1)
+    contract = (((1,), (1,)), ((), ()))
     out_ref[...] = lax.dot_general(
-        out_ref[...],
-        inverse[...],
-        (((1,), (1,)), ((), ())),
-        precision=HIGHEST,
-        preferred_element_type=jnp.float32,
+        parts[...], wide, contract, preferred_element_type=jnp.float32
+    ) + lax.dot_general(
+        parts[:, :width], inverse_low, contract, preferred_element_type=jnp.float32
     )
 
 
@@ -456,12 +475,14 @@
         vmem((2, 2, faces, width), jnp.bfloat16),
         vmem((2, 2, faces, width), jnp.bfloat16),
         [pltpu.SemaphoreType.DMA((2, messages))] * 2,
+        vmem((locked, nodes), jnp.bfloat16),
         vmem((locked, width), jnp.float32),
         sum_scratch(sizes, locked, width),
         vmem((count(locked), locked // count(locked), width), jnp.bfloat16),
         vmem((width, width), jnp.float32),
         sum_scratch(sizes, width, width),
         vmem((count(width), width // count(width), width), jnp.float32),
+        vmem((nodes, 2 * width), jnp.bfloat16),
         vmem((width, width), jnp.float32),
         vmem((width, width), jnp.float32),
     ]

time: 94.9 us -> 93.3 us (0.983)
  Pallas kernels: 92.5 us -> 90.9 us
    pallas_call x1, Pallas kernels: 92.5 us -> 90.9 us  [per_device(): pl.pallas_call(functools.partial(kernel, sizes, cells, nodes_total), out_...]
where the time goes in v3:
time: 93.3 us; the launch traced here: 93.2 us
  Pallas kernels  90.9 us (97%)
  local copies, waits for them, and re-layouts  2.22 us (2%)
    pallas_call x1, Pallas kernels, per_device(): pl.pallas_call(functools.partial(kernel, sizes, cells, nodes_total), out_...  90.9 us
    unnamed x8, local copies, waits for them, and re-layouts  2.22 us

profile of v3, /device:TPU:0, one launch (start us, length us, event | category | flops | bytes accessed | tf_op | source)
XLA Modules:
  0.0 93.2 jit_solution(2267476660250912335)
XLA Ops:
  0.0 0.0 copy-start.2
  0.0 0.0 copy-start
  0.0 0.0 copy-start.1
  0.0 1.4 %copy.7 = bf16[1,1,4,343,343]{4,3,2,1,0:T(8,128)(2,1)S(1)} copy(bf16[1,1,4,343,343]{4,2,3,1,0:T(4,128)(2,1)} %param.6) | data formatting | bytes 1882384 | tf_op args[2]
  1.5 0.0 copy-done.2
  1.5 0.0 copy-done
  1.5 0.0 copy-done.1
  1.5 90.9 %shard_map.46 = f32[864,128]{1,0:T(8,128)S(1)} custom-call(f32[7,3]{1,0:T(8,128)S(1)} %copy-done.2, bf16[6,6,24,128]{3,2,1,0:T(8,128)(2,1)S(1)} %copy-done.1, bf16[864,384]{1,0:T(8,128)(2,1)S(1)} %bitcast.7, bf16[4,343,343]{2,1,0:T(8,128)(2,1)S(1)} %bitcast.5), custom_call_target="tpu_custom_call" | custom-call | tf_op jit(solution)/shard_map/pallas_call | solution.py:489
  92.4 0.8 copy.9
Async XLA Ops:
  0.0 1.5 %copy-start.2 = (f32[7,3]{1,0:T(8,128)S(1)}, f32[7,3]{1,0:T(8,128)}, u32[]{:S(2)}) copy-start(f32[7,3]{1,0:T(8,128)} %constant.2.clone.coef_ref) | copy-start | bytes 256
  0.0 1.5 %copy-start = (bf16[6,6,24,384]{3,2,1,0:T(8,128)(2,1)S(1)}, bf16[6,6,24,384]{3,2,1,0:T(8,128)(2,1)}, u32[]{:S(2)}) copy-start(bf16[6,6,24,384]{3,2,1,0:T(8,128)(2,1)} %param.5) | copy-start | bytes 1990660
  0.0 1.5 %copy-start.1 = (bf16[6,6,24,128]{3,2,1,0:T(8,128)(2,1)S(1)}, bf16[6,6,24,128]{3,2,1,0:T(8,128)(2,1)}, u32[]{:S(2)}) copy-start(bf16[6,6,24,128]{3,2,1,0:T(8,128)(2,1)} %start_ref.1) | copy-start | bytes 663556

commit v4 on v3

--- a/solution.py
+++ b/solution.py
@@ -311,7 +311,8 @@
     start_ref,
     locked_ref,
     h_ref,
-    out_ref,
+    parts,
+    gram_rows,
     padded_h,
     grid_nodes,
     state,
@@ -327,10 +328,6 @@
     coefficient,
     gram_part,
     gram_scratch,
-    gram_rows,
-    parts,
-    mixed,
-    inverse,
 ):
     width = work.shape[1]
     node = h_ref.shape[1]
@@ -441,6 +438,10 @@
         + terms[width:, width:]
     )
     sum_over_devices(sizes, gram_part, gram_scratch, lambda total: total / nodes_total, gram_rows)
+
+
+def finish_kernel(parts, gram_rows, out_ref, mixed, inverse):
+    width = out_ref.shape[1]
     inverse_factor(gram_rows[...].reshape(width, width), mixed, inverse)
     inverse_high, inverse_low = split(inverse[...])
     wide = jnp.concatenate([inverse_high, inverse_high], axis=1)
@@ -481,17 +482,17 @@
         vmem((count(locked), locked // count(locked), width), jnp.bfloat16),
         vmem((width, width), jnp.float32),
         sum_scratch(sizes, width, width),
-        vmem((count(width), width // count(width), width), jnp.float32),
-        vmem((nodes, 2 * width), jnp.bfloat16),
-        vmem((width, width), jnp.float32),
-        vmem((width, width), jnp.float32),
     ]
-    result = pl.pallas_call(
+    block = pl.BlockSpec(memory_space=pltpu.VMEM)
+    parts, gram = pl.pallas_call(
         functools.partial(kernel, sizes, cells, nodes_total),
-        out_shape=jax.ShapeDtypeStruct((nodes, width), jnp.float32),
+        out_shape=(
+            jax.ShapeDtypeStruct((nodes, 2 * width), jnp.bfloat16),
+            jax.ShapeDtypeStruct((count(width), width // count(width), width), jnp.float32),
+        ),
         in_specs=[pl.BlockSpec(memory_space=pltpu.SMEM)]
-        + [pl.BlockSpec(memory_space=pltpu.VMEM)] * 3,
-        out_specs=pl.BlockSpec(memory_space=pltpu.VMEM),
+        + [block] * 3,
+        out_specs=(block, block),
         scratch_shapes=scratch,
         compiler_params=pltpu.CompilerParams(
             collective_id=0, has_side_effects=True, vmem_limit_bytes=40 << 20
@@ -502,6 +503,14 @@
         locked_orbitals.reshape(nodes, locked),
         cell_h.reshape(cell_h.shape[2:]),
     )
+    result = pl.pallas_call(
+        finish_kernel,
+        out_shape=jax.ShapeDtypeStruct((nodes, width), jnp.float32),
+        in_specs=[block, block],
+        out_specs=block,
+        scratch_shapes=[vmem((width, width), jnp.float32), vmem((width, width), jnp.float32)],
+        compiler_params=pltpu.CompilerParams(vmem_limit_bytes=16 << 20),
+    )(parts, gram)
     return result.reshape(start_block.shape)
 
 

time: 93.3 us -> 93.3 us (level)
    pallas_call x0 -> x1, Pallas kernels: none -> 5.56 us  [per_device(): pl.pallas_call(finish_kernel, out_shape=jax.ShapeDtypeStruct((nodes, widt...]
    pallas_call x1, Pallas kernels: 90.9 us -> 86.1 us  [per_device(): pl.pallas_call(functools.partial(kernel, sizes, cells, nodes_total), out_...]
    unnamed x8 -> x7, local copies, waits for them, and re-layouts: 2.22 us -> 1.45 us
where the time goes in v4:
time: 93.3 us; the launch traced here: 93.1 us
  Pallas kernels  91.6 us (98%)
  local copies, waits for them, and re-layouts  1.45 us (2%)
    pallas_call x1, Pallas kernels, per_device(): pl.pallas_call(functools.partial(kernel, sizes, cells, nodes_total), out_...  86.1 us
    pallas_call x1, Pallas kernels, per_device(): pl.pallas_call(finish_kernel, out_shape=jax.ShapeDtypeStruct((nodes, widt...  5.56 us

profile of v4, /device:TPU:0, one launch (start us, length us, event | category | flops | bytes accessed | tf_op | source)
XLA Modules:
  0.0 93.1 jit_solution(2658498066089712460)
XLA Ops:
  0.0 0.0 copy-start.2
  0.0 0.0 copy-start
  0.0 0.0 copy-start.1
  0.0 1.4 %copy.7 = bf16[1,1,4,343,343]{4,3,2,1,0:T(8,128)(2,1)S(1)} copy(bf16[1,1,4,343,343]{4,2,3,1,0:T(4,128)(2,1)} %param.6) | data formatting | bytes 1882384 | tf_op args[2]
  1.5 0.0 copy-done.2
  1.5 0.0 copy-done
  1.5 0.0 copy-done.1
  1.5 86.1 %shard_map.46 = (bf16[864,256]{1,0:T(8,128)(2,1)S(1)}, f32[8,16,128]{2,1,0:T(8,128)S(1)}) custom-call(f32[7,3]{1,0:T(8,128)S(1)} %copy-done.2, bf16[6,6,24,128]{3,2,1,0:T(8,128)(2,1)S(1)} %copy-done.1, bf16[864,384]{1,0:T(8,128)(2,1)S(1)} %bitcast.6, bf16[4,343,343]{2,1,0:T(8,128)(2,1)S(1)} %bitcast.5), custom_call_target="tpu_custom_call" | custom-call | tf_op jit(solution)/shard_map/pallas_call | solution.py:487
  87.6 5.6 %shard_map.47 = f32[864,128]{1,0:T(8,128)} custom-call(bf16[864,256]{1,0:T(8,128)(2,1)S(1)} %get-tuple-element.7.parts, f32[8,16,128]{2,1,0:T(8,128)S(1)} %get-tuple-element.8.gram_rows), custom_call_target="tpu_custom_call" | custom-call | tf_op jit(solution)/shard_map/pallas_call | solution.py:506
Async XLA Ops:
  0.0 1.5 %copy-start.2 = (f32[7,3]{1,0:T(8,128)S(1)}, f32[7,3]{1,0:T(8,128)}, u32[]{:S(2)}) copy-start(f32[7,3]{1,0:T(8,128)} %constant.2.clone.coef_ref) | copy-start | bytes 256
  0.0 1.5 %copy-start = (bf16[6,6,24,384]{3,2,1,0:T(8,128)(2,1)S(1)}, bf16[6,6,24,384]{3,2,1,0:T(8,128)(2,1)}, u32[]{:S(2)}) copy-start(bf16[6,6,24,384]{3,2,1,0:T(8,128)(2,1)} %param.5) | copy-start | bytes 1990660
  0.0 1.5 %copy-start.1 = (bf16[6,6,24,128]{3,2,1,0:T(8,128)(2,1)S(1)}, bf16[6,6,24,128]{3,2,1,0:T(8,128)(2,1)}, u32[]{:S(2)}) copy-start(bf16[6,6,24,128]{3,2,1,0:T(8,128)(2,1)} %start_ref.1) | copy-start | bytes 663556

commit v5 on v4

--- a/solution.py
+++ b/solution.py
@@ -175,14 +175,15 @@
 
 
 class Halo:
-    def __init__(self, sizes, cells, work, z_send, z_recv, f_send, f_recv, sems):
-        self.sizes, self.cells, self.work = sizes, cells, work
+    def __init__(self, sizes, half, pairs, work, z_send, z_recv, f_send, f_recv, sems, places):
+        self.half, self.pairs, self.work = half, pairs, work
         self.z_send, self.z_recv = z_send, z_recv
         self.f_send, self.f_recv = f_send, f_recv
         self.send_sem, self.recv_sem = sems
         self.messages = merged(sizes)
-        steps = Z_STEPS + tuple(steps[0] for steps in self.messages)
-        self.places = {step: neighbour(sizes, step) for step in steps}
+        self.places = places
+        self.side = work.shape[1] // 2
+        self.low = lax.broadcasted_iota(jnp.int32, (LINES, work.shape[1]), 1) < self.side
 
     def remote(self, slot, number, step, source, target):
         return pltpu.make_async_remote_copy(
@@ -204,73 +205,88 @@
             rows = [side_of(step[0])]
         return [pl.ds(first + (a * SIDE + side_of(step[1])) * TILE, TILE) for a in rows]
 
-    def send_faces(self, slot, group, cells):
+    def face_copies(self, slot):
         copies = []
         row = 0
         for n, steps in enumerate(self.messages):
-            begin = row
-            for step in steps:
-                part = [self.work[at, :] for k in cells for at in self.lines(k, step)]
-                size = part_rows(step, len(cells))
-                self.f_send[slot, group, row : row + size, :] = jnp.concatenate(part, 0).astype(
-                    self.f_send.dtype
-                )
-                row += size
-            rows = pl.ds(begin, row - begin)
+            size = sum(part_rows(step, self.pairs) for step in steps)
+            rows = pl.ds(row, size)
+            row += size
             copies.append(
                 self.remote(
                     slot,
-                    len(Z_STEPS) + group * len(self.messages) + n,
+                    2 * len(Z_STEPS) + self.half * len(self.messages) + n,
                     steps[0],
-                    self.f_send.at[slot, group, rows],
-                    self.f_recv.at[slot, group, rows],
+                    self.f_send.at[slot, self.half, rows],
+                    self.f_recv.at[slot, self.half, rows],
                 )
             )
-            copies[-1].start()
         return copies
 
-    def add_faces(self, slot, group, cells, copies):
+    def send_faces(self, slot):
         row = 0
-        for copy, steps in zip(copies, self.messages):
+        for copy, steps in zip(self.face_copies(slot), self.messages):
+            for step in steps:
+                part = [self.work[at, :] for k in range(self.pairs) for at in self.lines(k, step)]
+                size = part_rows(step, self.pairs)
+                self.f_send[slot, self.half, row : row + size, :] = jnp.concatenate(
+                    part, 0
+                ).astype(self.f_send.dtype)
+                row += size
+            copy.start()
+
+    def add_faces(self, slot):
+        row = 0
+        for copy, steps in zip(self.face_copies(slot), self.messages):
             copy.wait()
             for step in steps:
-                size = part_rows(step, len(cells))
-                got = self.f_recv[slot, group, row : row + size, :].astype(jnp.float32)
+                size = part_rows(step, self.pairs)
+                got = self.f_recv[slot, self.half, row : row + size, :].astype(jnp.float32)
                 row += size
                 taken = 0
-                for k in cells:
+                for k in range(self.pairs):
                     for at in self.lines(k, tuple(-d for d in step)):
                         self.work[at, :] = self.work[at, :] + got[taken : taken + at.size]
                         taken += at.size
 
-    def z_rows(self, cell, c):
-        return pl.ds(cell * CELL_ROWS + c, LINES, stride=TILE)
+    def z_rows(self, pair, c):
+        return pl.ds(pair * CELL_ROWS + c, LINES, stride=TILE)
 
     def z_copies(self, slot):
+        first = self.half * len(Z_STEPS)
         return [
             self.remote(slot, n, step, self.z_send.at[slot, n], self.z_recv.at[slot, n])
-            for n, step in enumerate(Z_STEPS)
+            for n, step in enumerate(Z_STEPS, first)
         ]
 
     def send_z(self, slot):
         work = self.work
-        self.z_send[slot, 0] = work[self.z_rows(self.cells - 1, ORDER), :]
-        self.z_send[slot, 1] = work[self.z_rows(0, 0), :]
+        first = self.half * len(Z_STEPS)
+        bottom_rows, top_rows = self.z_rows(0, 0), self.z_rows(self.pairs - 1, ORDER)
+        bottom, top = work[bottom_rows, :], pltpu.roll(work[top_rows, :], self.side, 1)
+        self.z_send[slot, first] = top
+        self.z_send[slot, first + 1] = bottom
         for copy in self.z_copies(slot):
             copy.start()
-        for cell in range(self.cells - 1):
-            lower, upper = self.z_rows(cell, ORDER), self.z_rows(cell + 1, 0)
+        for pair in range(self.pairs - 1):
+            lower, upper = self.z_rows(pair, ORDER), self.z_rows(pair + 1, 0)
             both = work[lower, :] + work[upper, :]
             work[lower, :] = both
             work[upper, :] = both
+        both = bottom + top
+        work[bottom_rows, :] = jnp.where(self.low, bottom, both)
+        work[top_rows, :] = pltpu.roll(jnp.where(self.low, top, both), self.side, 1)
 
     def add_z(self, slot):
         work = self.work
+        first = self.half * len(Z_STEPS)
         for copy in self.z_copies(slot):
             copy.wait()
-        bottom, top = self.z_rows(0, 0), self.z_rows(self.cells - 1, ORDER)
-        work[bottom, :] = work[bottom, :] + self.z_recv[slot, 0]
-        work[top, :] = work[top, :] + self.z_recv[slot, 1]
+        bottom, top = self.z_rows(0, 0), self.z_rows(self.pairs - 1, ORDER)
+        below = jnp.where(self.low, self.z_recv[slot, first], 0.0)
+        above = jnp.where(self.low, self.z_recv[slot, first + 1], 0.0)
+        work[bottom, :] = work[bottom, :] + below
+        work[top, :] = work[top, :] + pltpu.roll(above, self.side, 1)
 
 
 def inverse_factor(gram, mixed, inverse):
@@ -329,8 +345,9 @@
     gram_part,
     gram_scratch,
 ):
-    width = work.shape[1]
+    width = work.shape[2]
     node = h_ref.shape[1]
+    pairs = cells // 2
     steps = greeted(sizes, [groups(sizes, locked_ref.shape[1])[0], groups(sizes, width)[0], *[(a,) for a in AXES]])
     barrier = pltpu.get_barrier_semaphore()
     for step in steps:
@@ -342,41 +359,57 @@
     grid_nodes[...] = jnp.zeros_like(grid_nodes)
     grid_nodes[:, :, :own, :] = start_ref[...].astype(jnp.float32)
     work[...] = jnp.zeros_like(work)
-    sub = lax.broadcasted_iota(jnp.int32, (ORDER, TILE, width), 1)
-    for k in range(cells):
+    tile_rows = ORDER * TILE
+    side = width // 2
+    low = lax.broadcasted_iota(jnp.int32, (tile_rows, width), 1) < side
+    owned = lax.broadcasted_iota(jnp.int32, (tile_rows, width), 0) % TILE < ORDER
+    for p in range(pairs):
         for a in range(ORDER):
-            values = grid_nodes[a, :, ORDER * k : ORDER * k + TILE, :]
-            first = k * CELL_ROWS + a * SIDE * TILE
-            work[first : first + ORDER * TILE, :] = jnp.where(sub < ORDER, values, 0.0).reshape(
-                ORDER * TILE, width
-            )
+            lower, upper = [
+                grid_nodes[a, :, ORDER * k : ORDER * k + TILE, :].reshape(tile_rows, width)
+                for k in (p, p + pairs)
+            ]
+            first = p * CELL_ROWS + a * SIDE * TILE
+            one = jnp.where(low, lower, pltpu.roll(upper, side, 1))
+            two = jnp.where(low, pltpu.roll(lower, side, 1), upper)
+            work[0, first : first + tile_rows, :] = jnp.where(owned, one, 0.0)
+            work[1, first : first + tile_rows, :] = jnp.where(owned, two, 0.0)
     pl.semaphore_wait(barrier, len(steps))
-    halo = Halo(sizes, cells, work, z_send, z_recv, f_send, f_recv, halo_sems)
-    inner, outer = tuple(range(1, cells - 1)), (0, cells - 1)
+    places = {
+        step: neighbour(sizes, step)
+        for step in Z_STEPS + tuple(message[0] for message in merged(sizes))
+    }
+    halos = [
+        Halo(
+            sizes, h, pairs, work.at[h], z_send, z_recv, f_send, f_recv, halo_sems, places
+        )
+        for h in range(2)
+    ]
     state[...] = jnp.zeros(state.shape, jnp.float32)
-
-    def finish_faces(slot, inner_copies, outer_copies):
-        halo.add_faces(slot, 0, inner, inner_copies)
-        halo.add_faces(slot, 1, outer, outer_copies)
-        halo.send_z(slot)
-
-    def update(t, group):
+    low_lanes = lax.broadcasted_iota(jnp.int32, (CELL_ROWS, width), 1) < side
+
+    def update(t, h):
         now, old = lax.rem(t, 2), lax.rem(t + 1, 2)
         scale, shift, back = coef_ref[t, 0], coef_ref[t, 1], coef_ref[t, 2]
-        for k in group:
-            rows = pl.ds(k * CELL_ROWS, CELL_ROWS)
-            state[now, rows, :] = (
-                scale * (work[rows, :] - shift * state[old, rows, :]) - back * state[now, rows, :]
+        for p in range(pairs):
+            rows = pl.ds(p * CELL_ROWS, CELL_ROWS)
+            state[now, h, rows, :] = (
+                scale * (work[h, rows, :] - shift * state[old, h, rows, :])
+                - back * state[now, h, rows, :]
             )
 
-    def multiply(t, group):
-        for k in group:
-            rows = pl.ds(k * CELL_ROWS, CELL_ROWS)
-            values = state[lax.rem(t, 2), rows, :].astype(jnp.bfloat16)
-            work[rows, :] = jnp.dot(padded_h[k], values, preferred_element_type=jnp.float32)
-
-    inner_copies = halo.send_faces(0, 0, inner)
-    outer_copies = halo.send_faces(0, 1, outer)
+    def multiply(t, h):
+        for p in range(pairs):
+            rows = pl.ds(p * CELL_ROWS, CELL_ROWS)
+            values = state[lax.rem(t, 2), h, rows, :].astype(jnp.bfloat16)
+            lower, upper = [
+                jnp.dot(padded_h[k], values, preferred_element_type=jnp.float32)
+                for k in (p, p + pairs)
+            ]
+            work[h, rows, :] = jnp.where(low_lanes, lower, upper)
+
+    for halo in halos:
+        halo.send_faces(0)
     row = lax.broadcasted_iota(jnp.int32, (CELL_ROWS, node), 0)
     col = lax.broadcasted_iota(jnp.int32, (CELL_ROWS, node), 1)
     place = jnp.where(row % TILE < SIDE, row // TILE * SIDE + row % TILE, -1)
@@ -387,31 +420,36 @@
             tall, spread, (((1,), (1,)), ((), ())), preferred_element_type=jnp.float32
         ).astype(jnp.bfloat16)
     locked_t[...] = locked_ref[...].T
-    finish_faces(0, inner_copies, outer_copies)
 
     def apply(t, carry):
-        slot = lax.rem(t, 2)
-        update(t - 1, inner)
-        multiply(t - 1, inner)
-        inner_copies = halo.send_faces(slot, 0, inner)
-        halo.add_z(lax.rem(t - 1, 2))
-        update(t - 1, outer)
-        multiply(t - 1, outer)
-        outer_copies = halo.send_faces(slot, 1, outer)
-        finish_faces(slot, inner_copies, outer_copies)
+        slot, before = lax.rem(t, 2), lax.rem(t - 1, 2)
+        for h, halo in enumerate(halos):
+            halo.add_faces(before)
+            halo.send_z(before)
+            halo.add_z(before)
+            update(t - 1, h)
+            multiply(t - 1, h)
+            halo.send_faces(slot)
         return carry
 
     lax.fori_loop(1, APPLY + 1, apply, 0)
-    update(APPLY, inner)
-    halo.add_z(APPLY % 2)
-    update(APPLY, outer)
     last = APPLY % 2
+    for halo in halos:
+        halo.add_faces(last)
+        halo.send_z(last)
+    for h, halo in enumerate(halos):
+        halo.add_z(last)
+        update(APPLY, h)
     for k in range(cells):
+        p, upper = k % pairs, k >= pairs
         for a in range(ORDER):
-            first = k * CELL_ROWS + a * SIDE * TILE
-            grid_nodes[a, :, ORDER * k : ORDER * k + TILE, :] = state[
-                last, first : first + ORDER * TILE, :
-            ].reshape(ORDER, TILE, width)
+            first = p * CELL_ROWS + a * SIDE * TILE
+            one, two = [state[last, h, first : first + tile_rows, :] for h in range(2)]
+            if upper:
+                values = jnp.where(low, pltpu.roll(one, side, 1), two)
+            else:
+                values = jnp.where(low, one, pltpu.roll(two, side, 1))
+            grid_nodes[a, :, ORDER * k : ORDER * k + TILE, :] = values.reshape(ORDER, TILE, width)
     filtered = (
         grid_nodes[:, :, :own, :].reshape(ORDER * ORDER * own, width).astype(jnp.bfloat16)
     )
@@ -462,17 +500,18 @@
     nodes = ORDER * ORDER * own
     nodes_total = float(nodes * count_of(sizes, AXES))
     count = lambda rows: count_of(sizes, groups(sizes, rows)[0])
-    largest = max(cells - 2, 2)
-    faces = sum(part_rows(step, largest) for step in X_STEPS + Y_STEPS + XY_STEPS)
-    messages = len(Z_STEPS) + 2 * len(merged(sizes))
+    pairs = cells // 2
+    assert cells == 2 * pairs
+    faces = sum(part_rows(step, pairs) for step in X_STEPS + Y_STEPS + XY_STEPS)
+    messages = 2 * (len(Z_STEPS) + len(merged(sizes)))
     vmem = pltpu.VMEM
     scratch = [
         vmem((cells, CELL_ROWS, CELL_ROWS), jnp.bfloat16),
         vmem((ORDER, ORDER, own + TILE, width), jnp.float32),
-        vmem((2, cells * CELL_ROWS, width), jnp.float32),
-        vmem((cells * CELL_ROWS, width), jnp.float32),
-        vmem((2, 2, LINES, width), jnp.float32),
-        vmem((2, 2, LINES, width), jnp.float32),
+        vmem((2, 2, pairs * CELL_ROWS, width), jnp.float32),
+        vmem((2, pairs * CELL_ROWS, width), jnp.float32),
+        vmem((2, 4, LINES, width), jnp.float32),
+        vmem((2, 4, LINES, width), jnp.float32),
         vmem((2, 2, faces, width), jnp.bfloat16),
         vmem((2, 2, faces, width), jnp.bfloat16),
         [pltpu.SemaphoreType.DMA((2, messages))] * 2,

time: 93.3 us -> 98.2 us (1.053)
  Pallas kernels: 91.6 us -> 96.5 us
    pallas_call x1, Pallas kernels: 86.1 us -> 91 us  [per_device(): pl.pallas_call(functools.partial(kernel, sizes, cells, nodes_total), out_...]
where the time goes in v5:
time: 98.2 us; the launch traced here: 98 us
  Pallas kernels  96.5 us (98%)
  local copies, waits for them, and re-layouts  1.45 us (1%)
    pallas_call x1, Pallas kernels, per_device(): pl.pallas_call(functools.partial(kernel, sizes, cells, nodes_total), out_...  91 us
    pallas_call x1, Pallas kernels, per_device(): pl.pallas_call(finish_kernel, out_shape=jax.ShapeDtypeStruct((nodes, widt...  5.56 us

profile of v5, /device:TPU:0, one launch (start us, length us, event | category | flops | bytes accessed | tf_op | source)
XLA Modules:
  0.0 98.0 jit_solution(3163522120033486940)
XLA Ops:
  0.0 0.0 copy-start.2
  0.0 0.0 copy-start
  0.0 0.0 copy-start.1
  0.0 1.4 %copy.7 = bf16[1,1,4,343,343]{4,3,2,1,0:T(8,128)(2,1)S(1)} copy(bf16[1,1,4,343,343]{4,2,3,1,0:T(4,128)(2,1)} %param.6) | data formatting | bytes 1882384 | tf_op args[2]
  1.5 0.0 copy-done.2
  1.5 0.0 copy-done
  1.5 0.0 copy-done.1
  1.5 91.0 %shard_map.46 = (bf16[864,256]{1,0:T(8,128)(2,1)S(1)}, f32[8,16,128]{2,1,0:T(8,128)S(1)}) custom-call(f32[7,3]{1,0:T(8,128)S(1)} %copy-done.2, bf16[6,6,24,128]{3,2,1,0:T(8,128)(2,1)S(1)} %copy-done.1, bf16[864,384]{1,0:T(8,128)(2,1)S(1)} %bitcast.6, bf16[4,343,343]{2,1,0:T(8,128)(2,1)S(1)} %bitcast.5), custom_call_target="tpu_custom_call" | custom-call | tf_op jit(solution)/shard_map/pallas_call | solution.py:526
  92.5 5.6 %shard_map.47 = f32[864,128]{1,0:T(8,128)} custom-call(bf16[864,256]{1,0:T(8,128)(2,1)S(1)} %get-tuple-element.7.parts, f32[8,16,128]{2,1,0:T(8,128)S(1)} %get-tuple-element.8.gram_rows), custom_call_target="tpu_custom_call" | custom-call | tf_op jit(solution)/shard_map/pallas_call | solution.py:545
Async XLA Ops:
  0.0 1.5 %copy-start.2 = (f32[7,3]{1,0:T(8,128)S(1)}, f32[7,3]{1,0:T(8,128)}, u32[]{:S(2)}) copy-start(f32[7,3]{1,0:T(8,128)} %constant.2.clone.coef_ref) | copy-start | bytes 256
  0.0 1.5 %copy-start = (bf16[6,6,24,384]{3,2,1,0:T(8,128)(2,1)S(1)}, bf16[6,6,24,384]{3,2,1,0:T(8,128)(2,1)}, u32[]{:S(2)}) copy-start(bf16[6,6,24,384]{3,2,1,0:T(8,128)(2,1)} %param.5) | copy-start | bytes 1990660
  0.0 1.5 %copy-start.1 = (bf16[6,6,24,128]{3,2,1,0:T(8,128)(2,1)S(1)}, bf16[6,6,24,128]{3,2,1,0:T(8,128)(2,1)}, u32[]{:S(2)}) copy-start(bf16[6,6,24,128]{3,2,1,0:T(8,128)(2,1)} %start_ref.1) | copy-start | bytes 663556

commit v6 on v4

--- a/solution.py
+++ b/solution.py
@@ -135,37 +135,37 @@
         rows = lambda place: part.at[pl.ds(pl.multiple_of(place * chunk, chunk), chunk)]
         slots[me] = rows(me)[...]
         exchange(sizes, scattered, rows, slots, send_sem, recv_sem)
-        total = jnp.sum(slots[...], axis=0)
+        total = jnp.sum(slots[...].astype(jnp.float32), axis=0)
     else:
         me = 0
-        total = part[...]
+        total = part[...].astype(jnp.float32)
     for axis, (slots, send_sem, recv_sem) in zip(whole, scratch[1:-1]):
         place = lax.axis_index(axis)
-        slots[place] = total
+        slots[place] = total.astype(slots.dtype)
         exchange(sizes, (axis,), lambda _: slots.at[place], slots, send_sem, recv_sem)
-        total = jnp.sum(slots[...], axis=0)
+        total = jnp.sum(slots[...].astype(jnp.float32), axis=0)
     gathered[me] = finish(total)
     if scattered:
         send_sem, recv_sem = scratch[-1]
         exchange(sizes, scattered, lambda _: gathered.at[me], gathered, send_sem, recv_sem)
 
 
-def sum_scratch(sizes, rows, width):
+def sum_scratch(sizes, rows, width, dtype=jnp.float32):
     scattered, whole = groups(sizes, rows)
     count = count_of(sizes, scattered)
     chunk = rows // count
     sems = lambda n: [pltpu.SemaphoreType.DMA((max(n - 1, 1),))] * 2
-    shapes = [[pltpu.VMEM((count, chunk, width), jnp.float32)] + sems(count)]
+    shapes = [[pltpu.VMEM((count, chunk, width), dtype)] + sems(count)]
     for axis in whole:
         n = sizes[axis]
-        shapes.append([pltpu.VMEM((n, chunk, width), jnp.float32)] + sems(n))
+        shapes.append([pltpu.VMEM((n, chunk, width), dtype)] + sems(n))
     shapes.append(sems(count))
     return shapes
 
 
 def merged(sizes):
     found = {}
-    for step in X_STEPS + Y_STEPS + XY_STEPS:
+    for step in XY_STEPS + X_STEPS + Y_STEPS:
         found.setdefault(tuple(d % sizes[a] for a, d in zip(AXES, step)), []).append(step)
     return list(found.values())
 
@@ -415,7 +415,9 @@
     filtered = (
         grid_nodes[:, :, :own, :].reshape(ORDER * ORDER * own, width).astype(jnp.bfloat16)
     )
-    cross_part[...] = jnp.dot(locked_t[...], filtered, preferred_element_type=jnp.float32)
+    cross_part[...] = jnp.dot(
+        locked_t[...], filtered, preferred_element_type=jnp.float32
+    ).astype(cross_part.dtype)
     sum_over_devices(
         sizes,
         cross_part,
@@ -477,8 +479,8 @@
         vmem((2, 2, faces, width), jnp.bfloat16),
         [pltpu.SemaphoreType.DMA((2, messages))] * 2,
         vmem((locked, nodes), jnp.bfloat16),
-        vmem((locked, width), jnp.float32),
-        sum_scratch(sizes, locked, width),
+        vmem((locked, width), jnp.bfloat16),
+        sum_scratch(sizes, locked, width, jnp.bfloat16),
         vmem((count(locked), locked // count(locked), width), jnp.bfloat16),
         vmem((width, width), jnp.float32),
         sum_scratch(sizes, width, width),

time: 93.3 us -> 88.5 us (0.949)
  Pallas kernels: 91.6 us -> 86.9 us
    pallas_call x1, Pallas kernels: 86.1 us -> 81.3 us  [per_device(): pl.pallas_call(functools.partial(kernel, sizes, cells, nodes_total), out_...]
where the time goes in v6:
time: 88.5 us; the launch traced here: 88.4 us
  Pallas kernels  86.9 us (98%)
  local copies, waits for them, and re-layouts  1.45 us (2%)
    pallas_call x1, Pallas kernels, per_device(): pl.pallas_call(functools.partial(kernel, sizes, cells, nodes_total), out_...  81.3 us
    pallas_call x1, Pallas kernels, per_device(): pl.pallas_call(finish_kernel, out_shape=jax.ShapeDtypeStruct((nodes, widt...  5.56 us

profile of v6, /device:TPU:0, one launch (start us, length us, event | category | flops | bytes accessed | tf_op | source)
XLA Modules:
  0.0 88.4 jit_solution(18140541066209963566)
XLA Ops:
  0.0 0.0 copy-start.2
  0.0 0.0 copy-start
  0.0 0.0 copy-start.1
  0.0 1.4 %copy.7 = bf16[1,1,4,343,343]{4,3,2,1,0:T(8,128)(2,1)S(1)} copy(bf16[1,1,4,343,343]{4,2,3,1,0:T(4,128)(2,1)} %param.6) | data formatting | bytes 1882384 | tf_op args[2]
  1.5 0.0 copy-done.2
  1.5 0.0 copy-done
  1.5 0.0 copy-done.1
  1.5 81.3 %shard_map.46 = (bf16[864,256]{1,0:T(8,128)(2,1)S(1)}, f32[8,16,128]{2,1,0:T(8,128)S(1)}) custom-call(f32[7,3]{1,0:T(8,128)S(1)} %copy-done.2, bf16[6,6,24,128]{3,2,1,0:T(8,128)(2,1)S(1)} %copy-done.1, bf16[864,384]{1,0:T(8,128)(2,1)S(1)} %bitcast.6, bf16[4,343,343]{2,1,0:T(8,128)(2,1)S(1)} %bitcast.5), custom_call_target="tpu_custom_call" | custom-call | tf_op jit(solution)/shard_map/pallas_call | solution.py:489
  82.8 5.6 %shard_map.47 = f32[864,128]{1,0:T(8,128)} custom-call(bf16[864,256]{1,0:T(8,128)(2,1)S(1)} %get-tuple-element.7.parts, f32[8,16,128]{2,1,0:T(8,128)S(1)} %get-tuple-element.8.gram_rows), custom_call_target="tpu_custom_call" | custom-call | tf_op jit(solution)/shard_map/pallas_call | solution.py:508
Async XLA Ops:
  0.0 1.5 %copy-start.2 = (f32[7,3]{1,0:T(8,128)S(1)}, f32[7,3]{1,0:T(8,128)}, u32[]{:S(2)}) copy-start(f32[7,3]{1,0:T(8,128)} %constant.2.clone.coef_ref) | copy-start | bytes 256
  0.0 1.5 %copy-start = (bf16[6,6,24,384]{3,2,1,0:T(8,128)(2,1)S(1)}, bf16[6,6,24,384]{3,2,1,0:T(8,128)(2,1)}, u32[]{:S(2)}) copy-start(bf16[6,6,24,384]{3,2,1,0:T(8,128)(2,1)} %param.5) | copy-start | bytes 1990660
  0.0 1.5 %copy-start.1 = (bf16[6,6,24,128]{3,2,1,0:T(8,128)(2,1)S(1)}, bf16[6,6,24,128]{3,2,1,0:T(8,128)(2,1)}, u32[]{:S(2)}) copy-start(bf16[6,6,24,128]{3,2,1,0:T(8,128)(2,1)} %start_ref.1) | copy-start | bytes 663556

commit v7 on v6

--- a/solution.py
+++ b/solution.py
@@ -163,9 +163,9 @@
     return shapes
 
 
-def merged(sizes):
+def merged(sizes, wanted=lambda step: True):
     found = {}
-    for step in XY_STEPS + X_STEPS + Y_STEPS:
+    for step in filter(wanted, XY_STEPS + X_STEPS + Y_STEPS):
         found.setdefault(tuple(d % sizes[a] for a, d in zip(AXES, step)), []).append(step)
     return list(found.values())
 
@@ -181,7 +181,9 @@
         self.f_send, self.f_recv = f_send, f_recv
         self.send_sem, self.recv_sem = sems
         self.messages = merged(sizes)
-        steps = Z_STEPS + tuple(steps[0] for steps in self.messages)
+        self.down = merged(sizes, lambda step: max(step) <= 0)
+        self.up = merged(sizes, lambda step: min(step) >= 0)
+        steps = Z_STEPS + tuple(m[0] for m in self.messages + self.down + self.up)
         self.places = {step: neighbour(sizes, step) for step in steps}
 
     def remote(self, slot, number, step, source, target):
@@ -204,10 +206,10 @@
             rows = [side_of(step[0])]
         return [pl.ds(first + (a * SIDE + side_of(step[1])) * TILE, TILE) for a in rows]
 
-    def send_faces(self, slot, group, cells):
+    def send_faces(self, slot, group, cells, messages):
         copies = []
         row = 0
-        for n, steps in enumerate(self.messages):
+        for n, steps in enumerate(messages):
             begin = row
             for step in steps:
                 part = [self.work[at, :] for k in cells for at in self.lines(k, step)]
@@ -229,9 +231,9 @@
             copies[-1].start()
         return copies
 
-    def add_faces(self, slot, group, cells, copies):
+    def add_faces(self, slot, group, cells, copies, messages):
         row = 0
-        for copy, steps in zip(copies, self.messages):
+        for copy, steps in zip(copies, messages):
             copy.wait()
             for step in steps:
                 size = part_rows(step, len(cells))
@@ -355,9 +357,9 @@
     inner, outer = tuple(range(1, cells - 1)), (0, cells - 1)
     state[...] = jnp.zeros(state.shape, jnp.float32)
 
-    def finish_faces(slot, inner_copies, outer_copies):
-        halo.add_faces(slot, 0, inner, inner_copies)
-        halo.add_faces(slot, 1, outer, outer_copies)
+    def finish_faces(slot, inner_copies, outer_copies, messages):
+        halo.add_faces(slot, 0, inner, inner_copies, messages)
+        halo.add_faces(slot, 1, outer, outer_copies, messages)
         halo.send_z(slot)
 
     def update(t, group):
@@ -375,8 +377,8 @@
             values = state[lax.rem(t, 2), rows, :].astype(jnp.bfloat16)
             work[rows, :] = jnp.dot(padded_h[k], values, preferred_element_type=jnp.float32)
 
-    inner_copies = halo.send_faces(0, 0, inner)
-    outer_copies = halo.send_faces(0, 1, outer)
+    inner_copies = halo.send_faces(0, 0, inner, halo.down)
+    outer_copies = halo.send_faces(0, 1, outer, halo.down)
     row = lax.broadcasted_iota(jnp.int32, (CELL_ROWS, node), 0)
     col = lax.broadcasted_iota(jnp.int32, (CELL_ROWS, node), 1)
     place = jnp.where(row % TILE < SIDE, row // TILE * SIDE + row % TILE, -1)
@@ -387,21 +389,25 @@
             tall, spread, (((1,), (1,)), ((), ())), preferred_element_type=jnp.float32
         ).astype(jnp.bfloat16)
     locked_t[...] = locked_ref[...].T
-    finish_faces(0, inner_copies, outer_copies)
-
-    def apply(t, carry):
+    finish_faces(0, inner_copies, outer_copies, halo.down)
+
+    def apply(t, messages):
         slot = lax.rem(t, 2)
         update(t - 1, inner)
         multiply(t - 1, inner)
-        inner_copies = halo.send_faces(slot, 0, inner)
+        inner_copies = halo.send_faces(slot, 0, inner, messages)
         halo.add_z(lax.rem(t - 1, 2))
         update(t - 1, outer)
         multiply(t - 1, outer)
-        outer_copies = halo.send_faces(slot, 1, outer)
-        finish_faces(slot, inner_copies, outer_copies)
+        outer_copies = halo.send_faces(slot, 1, outer, messages)
+        finish_faces(slot, inner_copies, outer_copies, messages)
+
+    def repeat(t, carry):
+        apply(t, halo.messages)
         return carry
 
-    lax.fori_loop(1, APPLY + 1, apply, 0)
+    lax.fori_loop(1, APPLY, repeat, 0)
+    apply(APPLY, halo.up)
     update(APPLY, inner)
     halo.add_z(APPLY % 2)
     update(APPLY, outer)

time: 88.5 us -> 86.1 us (0.973)
  Pallas kernels: 86.9 us -> 84.4 us
    pallas_call x1, Pallas kernels: 81.3 us -> 78.9 us  [per_device(): pl.pallas_call(functools.partial(kernel, sizes, cells, nodes_total), out_...]
where the time goes in v7:
time: 86.1 us; the launch traced here: 85.9 us
  Pallas kernels  84.4 us (98%)
  local copies, waits for them, and re-layouts  1.45 us (2%)
    pallas_call x1, Pallas kernels, per_device(): pl.pallas_call(functools.partial(kernel, sizes, cells, nodes_total), out_...  78.9 us
    pallas_call x1, Pallas kernels, per_device(): pl.pallas_call(finish_kernel, out_shape=jax.ShapeDtypeStruct((nodes, widt...  5.56 us

profile of v7, /device:TPU:0, one launch (start us, length us, event | category | flops | bytes accessed | tf_op | source)
XLA Modules:
  0.0 85.9 jit_solution(10231059649381494467)
XLA Ops:
  0.0 0.0 copy-start.2
  0.0 0.0 copy-start
  0.0 0.0 copy-start.1
  0.0 1.4 %copy.7 = bf16[1,1,4,343,343]{4,3,2,1,0:T(8,128)(2,1)S(1)} copy(bf16[1,1,4,343,343]{4,2,3,1,0:T(4,128)(2,1)} %param.6) | data formatting | bytes 1882384 | tf_op args[2]
  1.5 0.0 copy-done.2
  1.5 0.0 copy-done
  1.5 0.0 copy-done.1
  1.5 78.9 %shard_map.46 = (bf16[864,256]{1,0:T(8,128)(2,1)S(1)}, f32[8,16,128]{2,1,0:T(8,128)S(1)}) custom-call(f32[7,3]{1,0:T(8,128)S(1)} %copy-done.2, bf16[6,6,24,128]{3,2,1,0:T(8,128)(2,1)S(1)} %copy-done.1, bf16[864,384]{1,0:T(8,128)(2,1)S(1)} %bitcast.6, bf16[4,343,343]{2,1,0:T(8,128)(2,1)S(1)} %bitcast.5), custom_call_target="tpu_custom_call" | custom-call | tf_op jit(solution)/shard_map/pallas_call | solution.py:495
  80.4 5.6 %shard_map.47 = f32[864,128]{1,0:T(8,128)} custom-call(bf16[864,256]{1,0:T(8,128)(2,1)S(1)} %get-tuple-element.7.parts, f32[8,16,128]{2,1,0:T(8,128)S(1)} %get-tuple-element.8.gram_rows), custom_call_target="tpu_custom_call" | custom-call | tf_op jit(solution)/shard_map/pallas_call | solution.py:514
Async XLA Ops:
  0.0 1.5 %copy-start.2 = (f32[7,3]{1,0:T(8,128)S(1)}, f32[7,3]{1,0:T(8,128)}, u32[]{:S(2)}) copy-start(f32[7,3]{1,0:T(8,128)} %constant.2.clone.coef_ref) | copy-start | bytes 256
  0.0 1.5 %copy-start = (bf16[6,6,24,384]{3,2,1,0:T(8,128)(2,1)S(1)}, bf16[6,6,24,384]{3,2,1,0:T(8,128)(2,1)}, u32[]{:S(2)}) copy-start(bf16[6,6,24,384]{3,2,1,0:T(8,128)(2,1)} %param.5) | copy-start | bytes 1990660
  0.0 1.5 %copy-start.1 = (bf16[6,6,24,128]{3,2,1,0:T(8,128)(2,1)S(1)}, bf16[6,6,24,128]{3,2,1,0:T(8,128)(2,1)}, u32[]{:S(2)}) copy-start(bf16[6,6,24,128]{3,2,1,0:T(8,128)(2,1)} %start_ref.1) | copy-start | bytes 663556

commit v8 on v7

--- a/solution.py
+++ b/solution.py
@@ -183,6 +183,7 @@
         self.messages = merged(sizes)
         self.down = merged(sizes, lambda step: max(step) <= 0)
         self.up = merged(sizes, lambda step: min(step) >= 0)
+        self.first = lax.axis_index("gx") == 0
         steps = Z_STEPS + tuple(m[0] for m in self.messages + self.down + self.up)
         self.places = {step: neighbour(sizes, step) for step in steps}
 
@@ -228,8 +229,22 @@
                     self.f_recv.at[slot, group, rows],
                 )
             )
-            copies[-1].start()
+            if n and steps[0][0] == -1 and messages[n - 1][0][0] == 1:
+                self.start_pair(copies[-2], copies[-1])
+            elif n + 1 == len(messages) or steps[0][0] != 1 or messages[n + 1][0][0] != -1:
+                copies[-1].start()
         return copies
+
+    def start_pair(self, upward, downward):
+        @pl.when(self.first)
+        def _():
+            downward.start()
+            upward.start()
+
+        @pl.when(jnp.logical_not(self.first))
+        def _():
+            upward.start()
+            downward.start()
 
     def add_faces(self, slot, group, cells, copies, messages):
         row = 0

time: 86.1 us -> 84.8 us (0.985)
  Pallas kernels: 84.4 us -> 83.2 us
    pallas_call x1, Pallas kernels: 78.9 us -> 77.6 us  [per_device(): pl.pallas_call(functools.partial(kernel, sizes, cells, nodes_total), out_...]
where the time goes in v8:
time: 84.8 us; the launch traced here: 84.7 us
  Pallas kernels  83.2 us (98%)
  local copies, waits for them, and re-layouts  1.45 us (2%)
    pallas_call x1, Pallas kernels, per_device(): pl.pallas_call(functools.partial(kernel, sizes, cells, nodes_total), out_...  77.6 us
    pallas_call x1, Pallas kernels, per_device(): pl.pallas_call(finish_kernel, out_shape=jax.ShapeDtypeStruct((nodes, widt...  5.56 us

profile of v8, /device:TPU:0, one launch (start us, length us, event | category | flops | bytes accessed | tf_op | source)
XLA Modules:
  0.0 84.7 jit_solution(3994369351802145182)
XLA Ops:
  0.0 0.0 copy-start.2
  0.0 0.0 copy-start
  0.0 0.0 copy-start.1
  0.0 1.4 %copy.7 = bf16[1,1,4,343,343]{4,3,2,1,0:T(8,128)(2,1)S(1)} copy(bf16[1,1,4,343,343]{4,2,3,1,0:T(4,128)(2,1)} %param.6) | data formatting | bytes 1882384 | tf_op args[2]
  1.5 0.0 copy-done.2
  1.5 0.0 copy-done
  1.5 0.0 copy-done.1
  1.5 77.6 %shard_map.46 = (bf16[864,256]{1,0:T(8,128)(2,1)S(1)}, f32[8,16,128]{2,1,0:T(8,128)S(1)}) custom-call(f32[7,3]{1,0:T(8,128)S(1)} %copy-done.2, bf16[6,6,24,128]{3,2,1,0:T(8,128)(2,1)S(1)} %copy-done.1, bf16[864,384]{1,0:T(8,128)(2,1)S(1)} %bitcast.6, bf16[4,343,343]{2,1,0:T(8,128)(2,1)S(1)} %bitcast.5), custom_call_target="tpu_custom_call" | custom-call | tf_op jit(solution)/shard_map/pallas_call | solution.py:510
  79.1 5.6 %shard_map.47 = f32[864,128]{1,0:T(8,128)} custom-call(bf16[864,256]{1,0:T(8,128)(2,1)S(1)} %get-tuple-element.7.parts, f32[8,16,128]{2,1,0:T(8,128)S(1)} %get-tuple-element.8.gram_rows), custom_call_target="tpu_custom_call" | custom-call | tf_op jit(solution)/shard_map/pallas_call | solution.py:529
Async XLA Ops:
  0.0 1.5 %copy-start.2 = (f32[7,3]{1,0:T(8,128)S(1)}, f32[7,3]{1,0:T(8,128)}, u32[]{:S(2)}) copy-start(f32[7,3]{1,0:T(8,128)} %constant.2.clone.coef_ref) | copy-start | bytes 256
  0.0 1.5 %copy-start = (bf16[6,6,24,384]{3,2,1,0:T(8,128)(2,1)S(1)}, bf16[6,6,24,384]{3,2,1,0:T(8,128)(2,1)}, u32[]{:S(2)}) copy-start(bf16[6,6,24,384]{3,2,1,0:T(8,128)(2,1)} %param.5) | copy-start | bytes 1990660
  0.0 1.5 %copy-start.1 = (bf16[6,6,24,128]{3,2,1,0:T(8,128)(2,1)S(1)}, bf16[6,6,24,128]{3,2,1,0:T(8,128)(2,1)}, u32[]{:S(2)}) copy-start(bf16[6,6,24,128]{3,2,1,0:T(8,128)(2,1)} %start_ref.1) | copy-start | bytes 663556
